TPU v7x, 256 devices: a whole 4x4x8 slice. The times are simulated.
256 devices in a mesh: seq: 64 (over z_hi, y, x), panel: 4 (over z_lo, core).
Axes of the slice: x: 4, y: 4, z: 8 (z_hi: 4, z_lo: 2; z = z_hi * 2 + z_lo), core: 2. Of those that a mesh axis runs over, the one named last changes fastest.
Arguments:
- tokens: bfloat16 [16384, 1024], P('seq', 'panel'), may hold values from -6 to 6
- cotangent: bfloat16 [16384, 1024], P('seq', 'panel'), may hold values from -6 to 6
- in_weight: bfloat16 [3, 1024, 1024], P(None, None, 'panel'), may hold values from -0.1875 to 0.1875
- short_kernel: float32 [3, 3, 1024], P(None, None, 'panel'), may hold values from -1 to 1
- skip_gain: float32 [1024], P('panel'), may hold values from 0.5 to 1.5
- long_filter: float32 [16384, 1024], P('seq', 'panel'), may hold values from -1.25 to 1.25
- out_weight: bfloat16 [1024, 1024], P('panel'), may hold values from -0.1875 to 0.1875
Outputs:
- block_out: bfloat16 [16384, 1024], P('seq', 'panel')
- token_grad: bfloat16 [16384, 1024], P('seq', 'panel')
All inputs are finite; a program needn't handle non-finite values.
Results may differ from a plain program's by a relative error of at most 0.007.
Values may be sent and summed in bfloat16 or wider, within the bound.
A program may use at most 64 MiB of HBM per device.

v0:
```python
import math

import jax
import jax.numpy as jnp
from jax import lax
from jax.sharding import PartitionSpec as P

HIGHEST = lax.Precision.HIGHEST


def partner(value, axis, stride):
    mask = 2**stride
    pairs = [(source, source ^ mask) for source in range(lax.axis_size(axis))]
    return lax.ppermute(value, axis, pairs)


def shifted(value, axis, steps):
    count = lax.axis_size(axis)
    initial, last = (max(0, -steps), min(count, count - steps))
    return lax.ppermute(value, axis, [(source, source + steps) for source in range(initial, last)])


def dft_tables(size_count):
    counter = jnp.arange(size_count, dtype=jnp.int32)
    product_mod = counter[:, None] * counter[None, :] % size_count
    phase_angle = -2.0 * math.pi / size_count * product_mod.astype(jnp.float32)
    return (jnp.cos(phase_angle), jnp.sin(phase_angle))


def apply_dft(real_part, imag_part, einsum_form, inverse, table_size=0):
    table_size = real_part.shape[1]
    cos_table, sin_table = dft_tables(table_size)
    cos_real = jnp.einsum(einsum_form, cos_table, real_part, precision=HIGHEST)
    sin_real = jnp.einsum(einsum_form, sin_table, real_part, precision=HIGHEST)
    cos_imag = jnp.einsum(einsum_form, cos_table, imag_part, precision=HIGHEST)
    sin_imag = jnp.einsum(einsum_form, sin_table, imag_part, precision=HIGHEST)
    if inverse:
        return (cos_real + sin_imag, cos_imag - sin_real)
    return (cos_real - sin_imag, cos_imag + sin_real)


def rotate(real_part, imag_part, phase_angle):
    cos_part = jnp.cos(phase_angle)
    sin_part = jnp.sin(phase_angle)
    return (
        real_part * cos_part - imag_part * sin_part,
        real_part * sin_part + imag_part * cos_part,
    )


def multiply(left_spec, right_spec, mirror):
    left_real, left_imag = left_spec
    right_real, right_imag = right_spec
    if mirror:
        right_imag = -right_imag
    return (
        left_real * right_real - left_imag * right_imag,
        left_real * right_imag + left_imag * right_real,
    )


def freq_index():
    shard_index = lax.axis_index("seq")
    bit_count = lax.axis_size("seq").bit_length() - 1
    reversed_index = jnp.zeros((), jnp.int32)
    for bit_pos in range(bit_count):
        reversed_index = reversed_index + shard_index // (1 << bit_pos) % 2 * (
            1 << bit_count - 1 - bit_pos
        )
    return reversed_index


def across_forward(real_part, imag_part):
    shard_count = lax.axis_size("seq")
    shard_index = lax.axis_index("seq")
    for bit_pos in reversed(range(shard_count.bit_length() - 1)):
        half_span = 1 << bit_pos
        partner_real, partner_imag = partner((real_part, imag_part), "seq", bit_pos)
        upper_side = shard_index // half_span % 2 == 1
        phase_angle = -math.pi / half_span * (shard_index % half_span).astype(jnp.float32)
        diff_real, diff_imag = rotate(
            partner_real - real_part, partner_imag - imag_part, phase_angle
        )
        real_part = jnp.where(upper_side, diff_real, real_part + partner_real)
        imag_part = jnp.where(upper_side, diff_imag, imag_part + partner_imag)
    return (real_part, imag_part)


def across_inverse(real_part, imag_part):
    shard_count = lax.axis_size("seq")
    shard_index = lax.axis_index("seq")
    for bit_pos in range(shard_count.bit_length() - 1):
        half_span = 1 << bit_pos
        partner_real, partner_imag = partner((real_part, imag_part), "seq", bit_pos)
        upper_side = shard_index // half_span % 2 == 1
        phase_angle = -math.pi / half_span * (shard_index % half_span).astype(jnp.float32)
        turned_real, turned_imag = rotate(partner_real, partner_imag, -phase_angle)
        own_real, own_imag = rotate(real_part, imag_part, -phase_angle)
        next_real = jnp.where(
            upper_side, 0.5 * (partner_real - own_real), 0.5 * (real_part + turned_real)
        )
        next_imag = jnp.where(
            upper_side, 0.5 * (partner_imag - own_imag), 0.5 * (imag_part + turned_imag)
        )
        real_part, imag_part = (next_real, next_imag)
    return (real_part, imag_part)


def half_phase(row_count, length):
    positions = lax.axis_index("seq") * row_count + jnp.arange(row_count, dtype=jnp.int32)
    return -math.pi / length * positions.astype(jnp.float32)


def twiddle_phase(row_count, length):
    twiddle = jnp.arange(row_count, dtype=jnp.int32) * freq_index() % length
    return (-2.0 * math.pi / length * twiddle.astype(jnp.float32))[None, :, None]


def transform(signal):
    row_count = signal.shape[0]
    length = row_count * lax.axis_size("seq")
    half_angle = half_phase(row_count, length)
    real_part = jnp.stack([signal, signal * jnp.cos(half_angle)[:, None]])
    imag_part = jnp.stack([jnp.zeros_like(signal), signal * jnp.sin(half_angle)[:, None]])
    real_part, imag_part = across_forward(real_part, imag_part)
    real_part, imag_part = rotate(real_part, imag_part, twiddle_phase(row_count, length))
    return apply_dft(real_part, imag_part, "km,emc->ekc", False)


def untransform(spectrum):
    real_part, imag_part = spectrum
    row_count = real_part.shape[1]
    length = row_count * lax.axis_size("seq")
    real_part, imag_part = apply_dft(real_part, imag_part, "km,emc->ekc", True)
    real_part, imag_part = rotate(real_part, imag_part, -twiddle_phase(row_count, length))
    real_part, imag_part = across_inverse(real_part, imag_part)
    half_angle = half_phase(row_count, length)
    odd_term = (
        real_part[1] * jnp.cos(half_angle)[:, None] + imag_part[1] * jnp.sin(half_angle)[:, None]
    )
    return (real_part[0] + odd_term) * (0.5 / row_count)


def local(tokens, cotangent, in_weight, short_kernel, skip_gain, long_filter, out_weight):
    row_count = tokens.shape[0]
    tap_count = short_kernel.shape[0]
    forward_fn, inverse_fn = (transform, untransform)
    full_tok, full_cot = (
        lax.all_gather(tokens, "panel", axis=1, tiled=True),
        lax.all_gather(cotangent, "panel", axis=1, tiled=True),
    )
    projected = jnp.einsum(
        "td,jdc->jtc", full_tok, in_weight, preferred_element_type=jnp.float32
    ).astype(jnp.bfloat16)
    before = shifted(projected[:, row_count - (tap_count - 1) :, :], "seq", 1)
    extended = jnp.concatenate([before, projected], axis=1).astype(jnp.float32)
    filtered = short_kernel[0][:, None, :] * extended[:, tap_count - 1 :, :]
    for tap_index in range(1, tap_count):
        filtered = (
            filtered
            + short_kernel[tap_index][:, None, :]
            * extended[:, tap_count - 1 - tap_index : tap_count - 1 - tap_index + row_count, :]
        )
    gate_out, gate_in, value_path = (filtered[0], filtered[1], filtered[2])
    signal = value_path * gate_in
    filt_spec = forward_fn(long_filter)
    conv_state = (
        inverse_fn(multiply(forward_fn(signal), filt_spec, False)) + skip_gain[None, :] * signal
    )
    gated_state = (conv_state * gate_out).astype(jnp.bfloat16)
    partial_value = jnp.dot(gated_state, out_weight, preferred_element_type=jnp.float32)
    block_out = lax.psum_scatter(partial_value, "panel", scatter_dimension=1, tiled=True).astype(
        jnp.bfloat16
    )
    grad_gated = lax.dot_general(
        full_cot, out_weight, (((1,), (1,)), ((), ())), preferred_element_type=jnp.float32
    )
    grad_gate_out = grad_gated * conv_state
    grad_state = grad_gated * gate_out
    grad_signal = (
        inverse_fn(multiply(forward_fn(grad_state), filt_spec, True))
        + skip_gain[None, :] * grad_state
    )
    grad_value = grad_signal * gate_in
    grad_gate_in = grad_signal * value_path
    upstream = jnp.stack([grad_gate_out, grad_gate_in, grad_value])
    after_rim = shifted(upstream[:, : tap_count - 1, :], "seq", -1)
    widened = jnp.concatenate([upstream, after_rim], axis=1)
    grad_projected = short_kernel[0][:, None, :] * widened[:, :row_count, :]
    for tap_index in range(1, tap_count):
        grad_projected = (
            grad_projected
            + short_kernel[tap_index][:, None, :] * widened[:, tap_index : tap_index + row_count, :]
        )
    grad_projected = grad_projected.astype(jnp.bfloat16)
    grad_partial = jnp.einsum(
        "jtc,jdc->td", grad_projected, in_weight, preferred_element_type=jnp.float32
    )
    token_grad = lax.psum_scatter(grad_partial, "panel", scatter_dimension=1, tiled=True).astype(
        jnp.bfloat16
    )
    return (block_out, token_grad)


def solution(mesh):
    placed = (
        P("seq", "panel"),
        P("seq", "panel"),
        P(None, None, "panel"),
        P(None, None, "panel"),
        P("panel"),
        P("seq", "panel"),
        P("panel", None),
    )
    return jax.shard_map(
        local,
        mesh=mesh,
        in_specs=placed,
        out_specs=(P("seq", "panel"), P("seq", "panel")),
        check_vma=False,
    )
```

profile of v0, /device:TPU:1, one launch (start us, length us, event | category | flops | bytes accessed | tf_op | source)
XLA Modules:
  0.0 1017.1 jit_solution(10181924146237431390)
XLA Ops:
  7.2 9.9 all_gather.6
  41.8 14.9 %collective-permute-done.14 = f32[2,256,256]{2,1,0:T(8,128)} collective-permute-done((f32[2,256,256]{2,1,0:T(8,128)}, f32[2,256,256]{2,1,0:T(8,128)}, u32[]{:S(2)}, u32[]{:S(2)}) %collective-permute-start.14) | collective-permute-done | bytes 524320 | tf_op jit(solution)/shard_map/ppermute | solution.py:14
  59.0 55.8 %collective-permute-start.15 = (f32[2,256,256]{2,1,0:T(8,128)}, f32[2,256,256]{2,1,0:T(8,128)S(1)}, u32[]{:S(2)}, u32[]{:S(2)}) collective-permute-start(f32[2,256,256]{2,1,0:T(8,128)} %get-tuple-element.66), channel_id=1, source_target_pairs={{0,64},{4,68},{8,72},{12,76},{16,80},{20,84},{24,88},{28,92},{32,9... | collective-permute-start | bytes 1572872 | tf_op jit(solution)/shard_map/ppermute | solution.py:14
  117.6 23.0 %collective-permute-start.3 = (f32[2,256,256]{2,1,0:T(8,128)}, f32[2,256,256]{2,1,0:T(8,128)}, u32[]{:S(2)}, u32[]{:S(2)}) collective-permute-start(f32[2,256,256]{2,1,0:T(8,128)} %get-tuple-element.68), channel_id=1, source_target_pairs={{0,64},{4,68},{8,72},{12,76},{16,80},{20,84},{24,88},{28,92},{32,9... | collective-permute-start | bytes 1572872 | tf_op jit(solution)/shard_map/ppermute | solution.py:14
  140.6 35.2 %collective-permute-done.15 = f32[2,256,256]{2,1,0:T(8,128)S(1)} collective-permute-done((f32[2,256,256]{2,1,0:T(8,128)}, f32[2,256,256]{2,1,0:T(8,128)S(1)}, u32[]{:S(2)}, u32[]{:S(2)}) %collective-permute-start.15) | collective-permute-done | bytes 524320 | tf_op jit(solution)/shard_map/ppermute | solution.py:14
  176.6 10.5 %collective-permute-done.16 = f32[2,256,256]{2,1,0:T(8,128)} collective-permute-done((f32[2,256,256]{2,1,0:T(8,128)}, f32[2,256,256]{2,1,0:T(8,128)}, u32[]{:S(2)}, u32[]{:S(2)}) %collective-permute-start.16) | collective-permute-done | bytes 524320 | tf_op jit(solution)/shard_map/ppermute | solution.py:14
  198.3 11.2 %collective-permute-done.4 = f32[2,256,256]{2,1,0:T(8,128)} collective-permute-done((f32[2,256,256]{2,1,0:T(8,128)}, f32[2,256,256]{2,1,0:T(8,128)}, u32[]{:S(2)}, u32[]{:S(2)}) %collective-permute-start.4) | collective-permute-done | bytes 524320 | tf_op jit(solution)/shard_map/ppermute | solution.py:14
  227.1 11.2 %collective-permute-done.6 = f32[2,256,256]{2,1,0:T(8,128)} collective-permute-done((f32[2,256,256]{2,1,0:T(8,128)}, f32[2,256,256]{2,1,0:T(8,128)}, u32[]{:S(2)}, u32[]{:S(2)}) %collective-permute-start.6) | collective-permute-done | bytes 524320 | tf_op jit(solution)/shard_map/ppermute | solution.py:14
  241.9 8.1 collective-permute-done.19
  249.9 11.2 %collective-permute-done.20 = f32[2,256,256]{2,1,0:T(8,128)} collective-permute-done((f32[2,256,256]{2,1,0:T(8,128)}, f32[2,256,256]{2,1,0:T(8,128)}, u32[]{:S(2)}, u32[]{:S(2)}) %collective-permute-start.20) | collective-permute-done | bytes 524320 | tf_op jit(solution)/shard_map/ppermute | solution.py:14
  272.4 11.2 %collective-permute-done.8 = f32[2,256,256]{2,1,0:T(8,128)} collective-permute-done((f32[2,256,256]{2,1,0:T(8,128)S(1)}, f32[2,256,256]{2,1,0:T(8,128)}, u32[]{:S(2)}, u32[]{:S(2)}) %collective-permute-start.8) | collective-permute-done | bytes 524320 | tf_op jit(solution)/shard_map/ppermute | solution.py:14
  291.6 9.1 collective-permute-done.10
  300.7 11.2 %collective-permute-done.9 = f32[2,256,256]{2,1,0:T(8,128)S(1)} collective-permute-done((f32[2,256,256]{2,1,0:T(8,128)S(1)}, f32[2,256,256]{2,1,0:T(8,128)S(1)}, u32[]{:S(2)}, u32[]{:S(2)}) %collective-permute-start.9) | collective-permute-done | bytes 524320 | tf_op jit(solution)/shard_map/ppermute | solution.py:14
  314.1 8.4 collective-permute-done.23
  322.5 11.2 %collective-permute-done.24 = f32[2,256,256]{2,1,0:T(8,128)S(1)} collective-permute-done((f32[2,256,256]{2,1,0:T(8,128)S(1)}, f32[2,256,256]{2,1,0:T(8,128)S(1)}, u32[]{:S(2)}, u32[]{:S(2)}) %collective-permute-start.24) | collective-permute-done | bytes 524320 | tf_op jit(solution)/shard_map/ppermute | solution.py:14
  345.0 11.2 %collective-permute-done.12 = f32[2,256,256]{2,1,0:T(8,128)S(1)} collective-permute-done((f32[2,256,256]{2,1,0:T(8,128)S(1)}, f32[2,256,256]{2,1,0:T(8,128)S(1)}, u32[]{:S(2)}, u32[]{:S(2)}) %collective-permute-start.12) | collective-permute-done | bytes 524320 | tf_op jit(solution)/shard_map/ppermute | solution.py:14
  372.6 10.2 %collective-permute-done.25 = f32[2,256,256]{2,1,0:T(8,128)S(1)} collective-permute-done((f32[2,256,256]{2,1,0:T(8,128)S(1)}, f32[2,256,256]{2,1,0:T(8,128)S(1)}, u32[]{:S(2)}, u32[]{:S(2)}) %collective-permute-start.25) | collective-permute-done | bytes 524320 | tf_op jit(solution)/shard_map/ppermute | solution.py:14
  382.9 11.2 %collective-permute-done.26 = f32[2,256,256]{2,1,0:T(8,128)S(1)} collective-permute-done((f32[2,256,256]{2,1,0:T(8,128)S(1)}, f32[2,256,256]{2,1,0:T(8,128)S(1)}, u32[]{:S(2)}, u32[]{:S(2)}) %collective-permute-start.26) | collective-permute-done | bytes 524320 | tf_op jit(solution)/shard_map/ppermute | solution.py:14
  398.7 9.6 collective-permute-done.27
  408.3 11.2 %collective-permute-done.28 = f32[2,256,256]{2,1,0:T(8,128)} collective-permute-done((f32[2,256,256]{2,1,0:T(8,128)S(1)}, f32[2,256,256]{2,1,0:T(8,128)}, u32[]{:S(2)}, u32[]{:S(2)}) %collective-permute-start.28) | collective-permute-done | bytes 524320 | tf_op jit(solution)/shard_map/ppermute | solution.py:14
  423.8 8.6 collective-permute-done.29
  432.5 11.2 %collective-permute-done.30 = f32[2,256,256]{2,1,0:T(8,128)} collective-permute-done((f32[2,256,256]{2,1,0:T(8,128)S(1)}, f32[2,256,256]{2,1,0:T(8,128)}, u32[]{:S(2)}, u32[]{:S(2)}) %collective-permute-start.30) | collective-permute-done | bytes 524320 | tf_op jit(solution)/shard_map/ppermute | solution.py:14
  458.0 10.5 %collective-permute-done.32 = f32[2,256,256]{2,1,0:T(8,128)} collective-permute-done((f32[2,256,256]{2,1,0:T(8,128)}, f32[2,256,256]{2,1,0:T(8,128)}, u32[]{:S(2)}, u32[]{:S(2)}) %collective-permute-start.32) | collective-permute-done | bytes 524320 | tf_op jit(solution)/shard_map/ppermute | solution.py:14
  473.8 34.4 %collective-permute-done.33 = f32[2,256,256]{2,1,0:T(8,128)} collective-permute-done((f32[2,256,256]{2,1,0:T(8,128)}, f32[2,256,256]{2,1,0:T(8,128)}, u32[]{:S(2)}, u32[]{:S(2)}) %collective-permute-start.33) | collective-permute-done | bytes 524320 | tf_op jit(solution)/shard_map/ppermute | solution.py:14
  508.2 11.2 %collective-permute-done.34 = f32[2,256,256]{2,1,0:T(8,128)} collective-permute-done((f32[2,256,256]{2,1,0:T(8,128)S(1)}, f32[2,256,256]{2,1,0:T(8,128)}, u32[]{:S(2)}, u32[]{:S(2)}) %collective-permute-start.34) | collective-permute-done | bytes 524320 | tf_op jit(solution)/shard_map/ppermute | solution.py:14
  527.7 45.0 %all_gather.7 = bf16[256,1024]{1,0:T(8,128)(2,1)S(1)} all-gather(bf16[256,256]{1,0:T(8,128)(2,1)S(1)} %copy-done.11), channel_id=1, replica_groups=mesh['seq'=64,'panel'=4] {'panel'}, dimensions={1}, use_global_device_ids=true | all-gather | bytes 655360 | tf_op jit(solution)/shard_map/all_gather | solution.py:150
  582.4 11.7 %collective-permute-done.37 = f32[2,256,256]{2,1,0:T(8,128)S(1)} collective-permute-done((f32[2,256,256]{2,1,0:T(8,128)S(1)}, f32[2,256,256]{2,1,0:T(8,128)S(1)}, u32[]{:S(2)}, u32[]{:S(2)}) %collective-permute-start.37) | collective-permute-done | bytes 524320 | tf_op jit(solution)/shard_map/ppermute | solution.py:14
  594.1 11.5 %collective-permute-done.38 = f32[2,256,256]{2,1,0:T(8,128)S(1)} collective-permute-done((f32[2,256,256]{2,1,0:T(8,128)S(1)}, f32[2,256,256]{2,1,0:T(8,128)S(1)}, u32[]{:S(2)}, u32[]{:S(2)}) %collective-permute-start.38) | collective-permute-done | bytes 524320 | tf_op jit(solution)/shard_map/ppermute | solution.py:14
  605.8 25.0 %collective-permute-start.39 = (f32[2,256,256]{2,1,0:T(8,128)S(1)}, f32[2,256,256]{2,1,0:T(8,128)S(1)}, u32[]{:S(2)}, u32[]{:S(2)}) collective-permute-start(f32[2,256,256]{2,1,0:T(8,128)S(1)} %get-tuple-element.64), channel_id=1, source_target_pairs={{0,64},{4,68},{8,72},{12,76},{16,80},{20,84},{24,88},{28,92},{32,9... | collective-permute-start | bytes 1572872 | tf_op jit(solution)/shard_map/ppermute | solution.py:14
  630.9 34.3 %collective-permute-done.39 = f32[2,256,256]{2,1,0:T(8,128)S(1)} collective-permute-done((f32[2,256,256]{2,1,0:T(8,128)S(1)}, f32[2,256,256]{2,1,0:T(8,128)S(1)}, u32[]{:S(2)}, u32[]{:S(2)}) %collective-permute-start.39) | collective-permute-done | bytes 524320 | tf_op jit(solution)/shard_map/ppermute | solution.py:14
  665.1 11.2 %collective-permute-done.40 = f32[2,256,256]{2,1,0:T(8,128)S(1)} collective-permute-done((f32[2,256,256]{2,1,0:T(8,128)S(1)}, f32[2,256,256]{2,1,0:T(8,128)S(1)}, u32[]{:S(2)}, u32[]{:S(2)}) %collective-permute-start.40) | collective-permute-done | bytes 524320 | tf_op jit(solution)/shard_map/ppermute | solution.py:14
  679.8 10.8 %collective-permute-done.41 = f32[2,256,256]{2,1,0:T(8,128)S(1)} collective-permute-done((f32[2,256,256]{2,1,0:T(8,128)S(1)}, f32[2,256,256]{2,1,0:T(8,128)S(1)}, u32[]{:S(2)}, u32[]{:S(2)}) %collective-permute-start.41) | collective-permute-done | bytes 524320 | tf_op jit(solution)/shard_map/ppermute | solution.py:14
  690.6 11.2 %collective-permute-done.42 = f32[2,256,256]{2,1,0:T(8,128)S(1)} collective-permute-done((f32[2,256,256]{2,1,0:T(8,128)S(1)}, f32[2,256,256]{2,1,0:T(8,128)S(1)}, u32[]{:S(2)}, u32[]{:S(2)}) %collective-permute-start.42) | collective-permute-done | bytes 524320 | tf_op jit(solution)/shard_map/ppermute | solution.py:14
  703.6 10.1 collective-permute-done.43
  713.7 11.2 %collective-permute-done.44 = f32[2,256,256]{2,1,0:T(8,128)S(1)} collective-permute-done((f32[2,256,256]{2,1,0:T(8,128)S(1)}, f32[2,256,256]{2,1,0:T(8,128)S(1)}, u32[]{:S(2)}, u32[]{:S(2)}) %collective-permute-start.44) | collective-permute-done | bytes 524320 | tf_op jit(solution)/shard_map/ppermute | solution.py:14
  728.2 9.1 collective-permute-done.45
  737.4 11.2 %collective-permute-done.46 = f32[2,256,256]{2,1,0:T(8,128)S(1)} collective-permute-done((f32[2,256,256]{2,1,0:T(8,128)S(1)}, f32[2,256,256]{2,1,0:T(8,128)S(1)}, u32[]{:S(2)}, u32[]{:S(2)}) %collective-permute-start.46) | collective-permute-done | bytes 524320 | tf_op jit(solution)/shard_map/ppermute | solution.py:14
  759.7 11.2 %collective-permute-done.48 = f32[2,256,256]{2,1,0:T(8,128)S(1)} collective-permute-done((f32[2,256,256]{2,1,0:T(8,128)S(1)}, f32[2,256,256]{2,1,0:T(8,128)S(1)}, u32[]{:S(2)}, u32[]{:S(2)}) %collective-permute-start.48) | collective-permute-done | bytes 524320 | tf_op jit(solution)/shard_map/ppermute | solution.py:14
  794.3 11.2 %collective-permute-done.50 = f32[2,256,256]{2,1,0:T(8,128)S(1)} collective-permute-done((f32[2,256,256]{2,1,0:T(8,128)S(1)}, f32[2,256,256]{2,1,0:T(8,128)S(1)}, u32[]{:S(2)}, u32[]{:S(2)}) %collective-permute-start.50) | collective-permute-done | bytes 524320 | tf_op jit(solution)/shard_map/ppermute | solution.py:14
  818.8 11.3 %collective-permute-done.52 = f32[2,256,256]{2,1,0:T(8,128)S(1)} collective-permute-done((f32[2,256,256]{2,1,0:T(8,128)S(1)}, f32[2,256,256]{2,1,0:T(8,128)S(1)}, u32[]{:S(2)}, u32[]{:S(2)}) %collective-permute-start.52) | collective-permute-done | bytes 524320 | tf_op jit(solution)/shard_map/ppermute | solution.py:14
  838.7 10.4 %collective-permute-done.54 = f32[2,256,256]{2,1,0:T(8,128)S(1)} collective-permute-done((f32[2,256,256]{2,1,0:T(8,128)S(1)}, f32[2,256,256]{2,1,0:T(8,128)S(1)}, u32[]{:S(2)}, u32[]{:S(2)}) %collective-permute-start.54) | collective-permute-done | bytes 524320 | tf_op jit(solution)/shard_map/ppermute | solution.py:14
  852.5 9.6 collective-permute-done.55
  862.1 9.4 collective-permute-done.56
  876.4 28.0 %collective-permute-done.57 = f32[2,256,256]{2,1,0:T(8,128)} collective-permute-done((f32[2,256,256]{2,1,0:T(8,128)}, f32[2,256,256]{2,1,0:T(8,128)}, u32[]{:S(2)}, u32[]{:S(2)}) %collective-permute-start.57) | collective-permute-done | bytes 524320 | tf_op jit(solution)/shard_map/ppermute | solution.py:14
  904.4 11.2 %collective-permute-done.58 = f32[2,256,256]{2,1,0:T(8,128)} collective-permute-done((f32[2,256,256]{2,1,0:T(8,128)S(1)}, f32[2,256,256]{2,1,0:T(8,128)}, u32[]{:S(2)}, u32[]{:S(2)}) %collective-permute-start.58) | collective-permute-done | bytes 524320 | tf_op jit(solution)/shard_map/ppermute | solution.py:14
  922.9 38.5 %collective-permute-done.59 = f32[2,256,256]{2,1,0:T(8,128)S(1)} collective-permute-done((f32[2,256,256]{2,1,0:T(8,128)S(1)}, f32[2,256,256]{2,1,0:T(8,128)S(1)}, u32[]{:S(2)}, u32[]{:S(2)}) %collective-permute-start.59) | collective-permute-done | bytes 524320 | tf_op jit(solution)/shard_map/ppermute | solution.py:14
  961.3 11.2 %collective-permute-done.60 = f32[2,256,256]{2,1,0:T(8,128)S(1)} collective-permute-done((f32[2,256,256]{2,1,0:T(8,128)S(1)}, f32[2,256,256]{2,1,0:T(8,128)S(1)}, u32[]{:S(2)}, u32[]{:S(2)}) %collective-permute-start.60) | collective-permute-done | bytes 524320 | tf_op jit(solution)/shard_map/ppermute | solution.py:14
  983.3 25.0 %reduce-scatter.5.cloned.1.call-done = f32[256,256]{1,0:T(8,128)} async-done(((f32[256,1024]{1,0:T(8,128)}), f32[256,256]{1,0:T(8,128)}) %reduce-scatter.5.cloned.1.call-update) | async-done | bytes 262160 | tf_op jit(solution)/shard_map/reduce_scatter | solution.py:199
  (211 shorter events, 248.9 us)
Async XLA Ops:
  7.2 974.5 %reduce-scatter.3.cloned.1.call-start = ((), (), s32[]{:S(2)}) async-start(), calls=%async_computation.2 | async-start | bytes 1310720 | tf_op jit(solution)/shard_map/reduce_scatter | solution.py:172
  21.3 20.4 %collective-permute-start.13 = (f32[2,256,256]{2,1,0:T(8,128)}, f32[2,256,256]{2,1,0:T(8,128)}, u32[]{:S(2)}, u32[]{:S(2)}) collective-permute-start(f32[2,256,256]{2,1,0:T(8,128)} %pad_maximum_fusion.3), channel_id=1, source_target_pairs={{0,128},{4,132},{8,136},{12,140},{16,144},{20,148},{24,152},{28,15... | collective-permute-start | bytes 1572872 | tf_op jit(solution)/shard_map/ppermute | solution.py:14
  28.3 28.4 %collective-permute-start.14 = (f32[2,256,256]{2,1,0:T(8,128)}, f32[2,256,256]{2,1,0:T(8,128)}, u32[]{:S(2)}, u32[]{:S(2)}) collective-permute-start(f32[2,256,256]{2,1,0:T(8,128)} %stack.57), channel_id=1, source_target_pairs={{0,128},{4,132},{8,136},{12,140},{16,144},{20,148},{24,152},{28,15... | collective-permute-start | bytes 1572872 | tf_op jit(solution)/shard_map/ppermute | solution.py:14
  31.7 83.3 %collective-permute-start.1 = (f32[2,256,256]{2,1,0:T(8,128)}, f32[2,256,256]{2,1,0:T(8,128)}, u32[]{:S(2)}, u32[]{:S(2)}) collective-permute-start(f32[2,256,256]{2,1,0:T(8,128)} %pad_maximum_fusion.2), channel_id=1, source_target_pairs={{0,128},{4,132},{8,136},{12,140},{16,144},{20,148},{24,152},{28,15... | collective-permute-start | bytes 1572872 | tf_op jit(solution)/shard_map/ppermute | solution.py:14
  38.7 76.3 %collective-permute-start.2 = (f32[2,256,256]{2,1,0:T(8,128)}, f32[2,256,256]{2,1,0:T(8,128)}, u32[]{:S(2)}, u32[]{:S(2)}) collective-permute-start(f32[2,256,256]{2,1,0:T(8,128)} %stack.52), channel_id=1, source_target_pairs={{0,128},{4,132},{8,136},{12,140},{16,144},{20,148},{24,152},{28,15... | collective-permute-start | bytes 1572872 | tf_op jit(solution)/shard_map/ppermute | solution.py:14
  59.0 116.7 %collective-permute-start.15 = (f32[2,256,256]{2,1,0:T(8,128)}, f32[2,256,256]{2,1,0:T(8,128)S(1)}, u32[]{:S(2)}, u32[]{:S(2)}) collective-permute-start(f32[2,256,256]{2,1,0:T(8,128)} %get-tuple-element.66), channel_id=1, source_target_pairs={{0,64},{4,68},{8,72},{12,76},{16,80},{20,84},{24,88},{28,92},{32,9... | collective-permute-start | bytes 1572872 | tf_op jit(solution)/shard_map/ppermute | solution.py:14
  114.8 72.3 %collective-permute-start.16 = (f32[2,256,256]{2,1,0:T(8,128)}, f32[2,256,256]{2,1,0:T(8,128)}, u32[]{:S(2)}, u32[]{:S(2)}) collective-permute-start(f32[2,256,256]{2,1,0:T(8,128)} %get-tuple-element.67), channel_id=1, source_target_pairs={{0,64},{4,68},{8,72},{12,76},{16,80},{20,84},{24,88},{28,92},{32,9... | collective-permute-start | bytes 1572872 | tf_op jit(solution)/shard_map/ppermute | solution.py:14
  117.6 80.8 %collective-permute-start.3 = (f32[2,256,256]{2,1,0:T(8,128)}, f32[2,256,256]{2,1,0:T(8,128)}, u32[]{:S(2)}, u32[]{:S(2)}) collective-permute-start(f32[2,256,256]{2,1,0:T(8,128)} %get-tuple-element.68), channel_id=1, source_target_pairs={{0,64},{4,68},{8,72},{12,76},{16,80},{20,84},{24,88},{28,92},{32,9... | collective-permute-start | bytes 1572872 | tf_op jit(solution)/shard_map/ppermute | solution.py:14
  140.5 69.1 %collective-permute-start.4 = (f32[2,256,256]{2,1,0:T(8,128)}, f32[2,256,256]{2,1,0:T(8,128)}, u32[]{:S(2)}, u32[]{:S(2)}) collective-permute-start(f32[2,256,256]{2,1,0:T(8,128)} %get-tuple-element.69), channel_id=1, source_target_pairs={{0,64},{4,68},{8,72},{12,76},{16,80},{20,84},{24,88},{28,92},{32,9... | collective-permute-start | bytes 1572872 | tf_op jit(solution)/shard_map/ppermute | solution.py:14
  188.8 26.4 %collective-permute-start.17 = (f32[2,256,256]{2,1,0:T(8,128)S(1)}, f32[2,256,256]{2,1,0:T(8,128)}, u32[]{:S(2)}, u32[]{:S(2)}) collective-permute-start(f32[2,256,256]{2,1,0:T(8,128)S(1)} %get-tuple-element.52), channel_id=1, source_target_pairs={{0,32},{4,36},{8,40},{12,44},{16,48},{20,52},{24,56},{28,60},{32,0... | collective-permute-start | bytes 1572872 | tf_op jit(solution)/shard_map/ppermute | solution.py:14
  191.8 23.4 %collective-permute-start.18 = (f32[2,256,256]{2,1,0:T(8,128)S(1)}, f32[2,256,256]{2,1,0:T(8,128)}, u32[]{:S(2)}, u32[]{:S(2)}) collective-permute-start(f32[2,256,256]{2,1,0:T(8,128)S(1)} %get-tuple-element.53), channel_id=1, source_target_pairs={{0,32},{4,36},{8,40},{12,44},{16,48},{20,52},{24,56},{28,60},{32,0... | collective-permute-start | bytes 1572872 | tf_op jit(solution)/shard_map/ppermute | solution.py:14
  215.2 23.2 %collective-permute-start.6 = (f32[2,256,256]{2,1,0:T(8,128)}, f32[2,256,256]{2,1,0:T(8,128)}, u32[]{:S(2)}, u32[]{:S(2)}) collective-permute-start(f32[2,256,256]{2,1,0:T(8,128)} %get-tuple-element.63), channel_id=1, source_target_pairs={{0,32},{4,36},{8,40},{12,44},{16,48},{20,52},{24,56},{28,60},{32,0... | collective-permute-start | bytes 1572872 | tf_op jit(solution)/shard_map/ppermute | solution.py:14
  217.7 32.3 %collective-permute-start.19 = (f32[2,256,256]{2,1,0:T(8,128)}, f32[2,256,256]{2,1,0:T(8,128)}, u32[]{:S(2)}, u32[]{:S(2)}) collective-permute-start(f32[2,256,256]{2,1,0:T(8,128)} %get-tuple-element.50), channel_id=1, source_target_pairs={{0,16},{4,20},{8,24},{12,28},{16,0},{20,4},{24,8},{28,12},{32,48},... | collective-permute-start | bytes 1572872 | tf_op jit(solution)/shard_map/ppermute | solution.py:14
  219.0 42.2 %collective-permute-start.20 = (f32[2,256,256]{2,1,0:T(8,128)}, f32[2,256,256]{2,1,0:T(8,128)}, u32[]{:S(2)}, u32[]{:S(2)}) collective-permute-start(f32[2,256,256]{2,1,0:T(8,128)} %get-tuple-element.51), channel_id=1, source_target_pairs={{0,16},{4,20},{8,24},{12,28},{16,0},{20,4},{24,8},{28,12},{32,48},... | collective-permute-start | bytes 1572872 | tf_op jit(solution)/shard_map/ppermute | solution.py:14
  240.1 32.3 %collective-permute-start.7 = (f32[2,256,256]{2,1,0:T(8,128)S(1)}, f32[2,256,256]{2,1,0:T(8,128)}, u32[]{:S(2)}, u32[]{:S(2)}) collective-permute-start(f32[2,256,256]{2,1,0:T(8,128)S(1)} %get-tuple-element.60), channel_id=1, source_target_pairs={{0,16},{4,20},{8,24},{12,28},{16,0},{20,4},{24,8},{28,12},{32,48},... | collective-permute-start | bytes 1572872 | tf_op jit(solution)/shard_map/ppermute | solution.py:14
  241.5 42.2 %collective-permute-start.8 = (f32[2,256,256]{2,1,0:T(8,128)S(1)}, f32[2,256,256]{2,1,0:T(8,128)}, u32[]{:S(2)}, u32[]{:S(2)}) collective-permute-start(f32[2,256,256]{2,1,0:T(8,128)S(1)} %get-tuple-element.61), channel_id=1, source_target_pairs={{0,16},{4,20},{8,24},{12,28},{16,0},{20,4},{24,8},{28,12},{32,48},... | collective-permute-start | bytes 1572872 | tf_op jit(solution)/shard_map/ppermute | solution.py:14
  263.9 24.2 %collective-permute-start.21 = (f32[2,256,256]{2,1,0:T(8,128)}, f32[2,256,256]{2,1,0:T(8,128)}, u32[]{:S(2)}, u32[]{:S(2)}) collective-permute-start(f32[2,256,256]{2,1,0:T(8,128)} %get-tuple-element.48), channel_id=1, source_target_pairs={{0,8},{4,12},{8,0},{12,4},{16,24},{20,28},{24,16},{28,20},{32,40},... | collective-permute-start | bytes 1572872 | tf_op jit(solution)/shard_map/ppermute | solution.py:14
  266.3 21.8 %collective-permute-start.22 = (f32[2,256,256]{2,1,0:T(8,128)}, f32[2,256,256]{2,1,0:T(8,128)}, u32[]{:S(2)}, u32[]{:S(2)}) collective-permute-start(f32[2,256,256]{2,1,0:T(8,128)} %get-tuple-element.49), channel_id=1, source_target_pairs={{0,8},{4,12},{8,0},{12,4},{16,24},{20,28},{24,16},{28,20},{32,40},... | collective-permute-start | bytes 1572872 | tf_op jit(solution)/shard_map/ppermute | solution.py:14
  287.6 24.3 %collective-permute-start.9 = (f32[2,256,256]{2,1,0:T(8,128)S(1)}, f32[2,256,256]{2,1,0:T(8,128)S(1)}, u32[]{:S(2)}, u32[]{:S(2)}) collective-permute-start(f32[2,256,256]{2,1,0:T(8,128)S(1)} %get-tuple-element.58), channel_id=1, source_target_pairs={{0,8},{4,12},{8,0},{12,4},{16,24},{20,28},{24,16},{28,20},{32,40},... | collective-permute-start | bytes 1572872 | tf_op jit(solution)/shard_map/ppermute | solution.py:14
  289.9 32.6 %collective-permute-start.23 = (f32[2,256,256]{2,1,0:T(8,128)S(1)}, f32[2,256,256]{2,1,0:T(8,128)S(1)}, u32[]{:S(2)}, u32[]{:S(2)}) collective-permute-start(f32[2,256,256]{2,1,0:T(8,128)S(1)} %get-tuple-element.46), channel_id=1, source_target_pairs={{0,4},{4,0},{8,12},{12,8},{16,20},{20,16},{24,28},{28,24},{32,36},... | collective-permute-start | bytes 1572872 | tf_op jit(solution)/shard_map/ppermute | solution.py:14
  291.2 42.5 %collective-permute-start.24 = (f32[2,256,256]{2,1,0:T(8,128)S(1)}, f32[2,256,256]{2,1,0:T(8,128)S(1)}, u32[]{:S(2)}, u32[]{:S(2)}) collective-permute-start(f32[2,256,256]{2,1,0:T(8,128)S(1)} %get-tuple-element.47), channel_id=1, source_target_pairs={{0,4},{4,0},{8,12},{12,8},{16,20},{20,16},{24,28},{28,24},{32,36},... | collective-permute-start | bytes 1572872 | tf_op jit(solution)/shard_map/ppermute | solution.py:14
  312.1 32.8 %collective-permute-start.11 = (f32[2,256,256]{2,1,0:T(8,128)S(1)}, f32[2,256,256]{2,1,0:T(8,128)S(1)}, u32[]{:S(2)}, u32[]{:S(2)}) collective-permute-start(f32[2,256,256]{2,1,0:T(8,128)S(1)} %get-tuple-element.56), channel_id=1, source_target_pairs={{0,4},{4,0},{8,12},{12,8},{16,20},{20,16},{24,28},{28,24},{32,36},... | collective-permute-start | bytes 1572872 | tf_op jit(solution)/shard_map/ppermute | solution.py:14
  313.4 42.8 %collective-permute-start.12 = (f32[2,256,256]{2,1,0:T(8,128)S(1)}, f32[2,256,256]{2,1,0:T(8,128)S(1)}, u32[]{:S(2)}, u32[]{:S(2)}) collective-permute-start(f32[2,256,256]{2,1,0:T(8,128)S(1)} %get-tuple-element.57), channel_id=1, source_target_pairs={{0,4},{4,0},{8,12},{12,8},{16,20},{20,16},{24,28},{28,24},{32,36},... | collective-permute-start | bytes 1572872 | tf_op jit(solution)/shard_map/ppermute | solution.py:14
  372.5 21.6 %collective-permute-start.26 = (f32[2,256,256]{2,1,0:T(8,128)S(1)}, f32[2,256,256]{2,1,0:T(8,128)S(1)}, u32[]{:S(2)}, u32[]{:S(2)}) collective-permute-start(f32[2,256,256]{2,1,0:T(8,128)S(1)} %get-tuple-element.72), channel_id=1, source_target_pairs={{0,4},{4,0},{8,12},{12,8},{16,20},{20,16},{24,28},{28,24},{32,36},... | collective-permute-start | bytes 1572872 | tf_op jit(solution)/shard_map/ppermute | solution.py:14
  397.8 21.7 %collective-permute-start.28 = (f32[2,256,256]{2,1,0:T(8,128)S(1)}, f32[2,256,256]{2,1,0:T(8,128)}, u32[]{:S(2)}, u32[]{:S(2)}) collective-permute-start(f32[2,256,256]{2,1,0:T(8,128)S(1)} %get-tuple-element.40), channel_id=1, source_target_pairs={{0,8},{4,12},{8,0},{12,4},{16,24},{20,28},{24,16},{28,20},{32,40},... | collective-permute-start | bytes 1572872 | tf_op jit(solution)/shard_map/ppermute | solution.py:14
  423.4 20.3 %collective-permute-start.30 = (f32[2,256,256]{2,1,0:T(8,128)S(1)}, f32[2,256,256]{2,1,0:T(8,128)}, u32[]{:S(2)}, u32[]{:S(2)}) collective-permute-start(f32[2,256,256]{2,1,0:T(8,128)S(1)} %get-tuple-element.38), channel_id=1, source_target_pairs={{0,16},{4,20},{8,24},{12,28},{16,0},{20,4},{24,8},{28,12},{32,48},... | collective-permute-start | bytes 1572872 | tf_op jit(solution)/shard_map/ppermute | solution.py:14
  448.3 20.3 %collective-permute-start.32 = (f32[2,256,256]{2,1,0:T(8,128)}, f32[2,256,256]{2,1,0:T(8,128)}, u32[]{:S(2)}, u32[]{:S(2)}) collective-permute-start(f32[2,256,256]{2,1,0:T(8,128)} %get-tuple-element.36), channel_id=1, source_target_pairs={{0,32},{4,36},{8,40},{12,44},{16,48},{20,52},{24,56},{28,60},{32,0... | collective-permute-start | bytes 1572872 | tf_op jit(solution)/shard_map/ppermute | solution.py:14
  471.2 37.0 %collective-permute-start.33 = (f32[2,256,256]{2,1,0:T(8,128)}, f32[2,256,256]{2,1,0:T(8,128)}, u32[]{:S(2)}, u32[]{:S(2)}) collective-permute-start(f32[2,256,256]{2,1,0:T(8,128)} %get-tuple-element.35), channel_id=1, source_target_pairs={{0,64},{4,68},{8,72},{12,76},{16,80},{20,84},{24,88},{28,92},{32,9... | collective-permute-start | bytes 1572872 | tf_op jit(solution)/shard_map/ppermute | solution.py:14
  471.2 48.2 %collective-permute-start.34 = (f32[2,256,256]{2,1,0:T(8,128)S(1)}, f32[2,256,256]{2,1,0:T(8,128)}, u32[]{:S(2)}, u32[]{:S(2)}) collective-permute-start(f32[2,256,256]{2,1,0:T(8,128)S(1)} %get-tuple-element.34), channel_id=1, source_target_pairs={{0,64},{4,68},{8,72},{12,76},{16,80},{20,84},{24,88},{28,92},{32,9... | collective-permute-start | bytes 1572872 | tf_op jit(solution)/shard_map/ppermute | solution.py:14
  522.1 50.5 %collective-permute-start.35 = (f32[2,256,256]{2,1,0:T(8,128)}, f32[2,256,256]{2,1,0:T(8,128)S(1)}, u32[]{:S(2)}, u32[]{:S(2)}) collective-permute-start(f32[2,256,256]{2,1,0:T(8,128)} %get-tuple-element.33), channel_id=1, source_target_pairs={{0,128},{4,132},{8,136},{12,140},{16,144},{20,148},{24,152},{28,15... | collective-permute-start | bytes 1572872 | tf_op jit(solution)/shard_map/ppermute | solution.py:14
  524.3 48.6 %collective-permute-start.36 = (f32[2,256,256]{2,1,0:T(8,128)}, f32[2,256,256]{2,1,0:T(8,128)}, u32[]{:S(2)}, u32[]{:S(2)}) collective-permute-start(f32[2,256,256]{2,1,0:T(8,128)} %get-tuple-element.32), channel_id=1, source_target_pairs={{0,128},{4,132},{8,136},{12,140},{16,144},{20,148},{24,152},{28,15... | collective-permute-start | bytes 1572872 | tf_op jit(solution)/shard_map/ppermute | solution.py:14
  576.8 17.3 %collective-permute-start.37 = (f32[2,256,256]{2,1,0:T(8,128)S(1)}, f32[2,256,256]{2,1,0:T(8,128)S(1)}, u32[]{:S(2)}, u32[]{:S(2)}) collective-permute-start(f32[2,256,256]{2,1,0:T(8,128)S(1)} %pad_maximum_fusion.4), channel_id=1, source_target_pairs={{0,128},{4,132},{8,136},{12,140},{16,144},{20,148},{24,152},{28,15... | collective-permute-start | bytes 1572872 | tf_op jit(solution)/shard_map/ppermute | solution.py:14
  580.6 25.0 %collective-permute-start.38 = (f32[2,256,256]{2,1,0:T(8,128)S(1)}, f32[2,256,256]{2,1,0:T(8,128)S(1)}, u32[]{:S(2)}, u32[]{:S(2)}) collective-permute-start(f32[2,256,256]{2,1,0:T(8,128)S(1)} %stack.63), channel_id=1, source_target_pairs={{0,128},{4,132},{8,136},{12,140},{16,144},{20,148},{24,152},{28,15... | collective-permute-start | bytes 1572872 | tf_op jit(solution)/shard_map/ppermute | solution.py:14
  605.8 59.3 %collective-permute-start.39 = (f32[2,256,256]{2,1,0:T(8,128)S(1)}, f32[2,256,256]{2,1,0:T(8,128)S(1)}, u32[]{:S(2)}, u32[]{:S(2)}) collective-permute-start(f32[2,256,256]{2,1,0:T(8,128)S(1)} %get-tuple-element.64), channel_id=1, source_target_pairs={{0,64},{4,68},{8,72},{12,76},{16,80},{20,84},{24,88},{28,92},{32,9... | collective-permute-start | bytes 1572872 | tf_op jit(solution)/shard_map/ppermute | solution.py:14
  630.8 45.6 %collective-permute-start.40 = (f32[2,256,256]{2,1,0:T(8,128)S(1)}, f32[2,256,256]{2,1,0:T(8,128)S(1)}, u32[]{:S(2)}, u32[]{:S(2)}) collective-permute-start(f32[2,256,256]{2,1,0:T(8,128)S(1)} %get-tuple-element.65), channel_id=1, source_target_pairs={{0,64},{4,68},{8,72},{12,76},{16,80},{20,84},{24,88},{28,92},{32,9... | collective-permute-start | bytes 1572872 | tf_op jit(solution)/shard_map/ppermute | solution.py:14
  676.8 25.1 %collective-permute-start.42 = (f32[2,256,256]{2,1,0:T(8,128)S(1)}, f32[2,256,256]{2,1,0:T(8,128)S(1)}, u32[]{:S(2)}, u32[]{:S(2)}) collective-permute-start(f32[2,256,256]{2,1,0:T(8,128)S(1)} %get-tuple-element.31), channel_id=1, source_target_pairs={{0,32},{4,36},{8,40},{12,44},{16,48},{20,52},{24,56},{28,60},{32,0... | collective-permute-start | bytes 1572872 | tf_op jit(solution)/shard_map/ppermute | solution.py:14
  702.4 22.6 %collective-permute-start.44 = (f32[2,256,256]{2,1,0:T(8,128)S(1)}, f32[2,256,256]{2,1,0:T(8,128)S(1)}, u32[]{:S(2)}, u32[]{:S(2)}) collective-permute-start(f32[2,256,256]{2,1,0:T(8,128)S(1)} %get-tuple-element.29), channel_id=1, source_target_pairs={{0,16},{4,20},{8,24},{12,28},{16,0},{20,4},{24,8},{28,12},{32,48},... | collective-permute-start | bytes 1572872 | tf_op jit(solution)/shard_map/ppermute | solution.py:14
  725.3 23.3 %collective-permute-start.46 = (f32[2,256,256]{2,1,0:T(8,128)S(1)}, f32[2,256,256]{2,1,0:T(8,128)S(1)}, u32[]{:S(2)}, u32[]{:S(2)}) collective-permute-start(f32[2,256,256]{2,1,0:T(8,128)S(1)} %get-tuple-element.27), channel_id=1, source_target_pairs={{0,8},{4,12},{8,0},{12,4},{16,24},{20,28},{24,16},{28,20},{32,40},... | collective-permute-start | bytes 1572872 | tf_op jit(solution)/shard_map/ppermute | solution.py:14
  751.8 19.2 %collective-permute-start.48 = (f32[2,256,256]{2,1,0:T(8,128)S(1)}, f32[2,256,256]{2,1,0:T(8,128)S(1)}, u32[]{:S(2)}, u32[]{:S(2)}) collective-permute-start(f32[2,256,256]{2,1,0:T(8,128)S(1)} %get-tuple-element.25), channel_id=1, source_target_pairs={{0,4},{4,0},{8,12},{12,8},{16,20},{20,16},{24,28},{28,24},{32,36},... | collective-permute-start | bytes 1572872 | tf_op jit(solution)/shard_map/ppermute | solution.py:14
  787.0 18.6 %collective-permute-start.50 = (f32[2,256,256]{2,1,0:T(8,128)S(1)}, f32[2,256,256]{2,1,0:T(8,128)S(1)}, u32[]{:S(2)}, u32[]{:S(2)}) collective-permute-start(f32[2,256,256]{2,1,0:T(8,128)S(1)} %get-tuple-element.70), channel_id=1, source_target_pairs={{0,4},{4,0},{8,12},{12,8},{16,20},{20,16},{24,28},{28,24},{32,36},... | collective-permute-start | bytes 1572872 | tf_op jit(solution)/shard_map/ppermute | solution.py:14
  812.0 18.2 %collective-permute-start.52 = (f32[2,256,256]{2,1,0:T(8,128)S(1)}, f32[2,256,256]{2,1,0:T(8,128)S(1)}, u32[]{:S(2)}, u32[]{:S(2)}) collective-permute-start(f32[2,256,256]{2,1,0:T(8,128)S(1)} %get-tuple-element.18), channel_id=1, source_target_pairs={{0,8},{4,12},{8,0},{12,4},{16,24},{20,28},{24,16},{28,20},{32,40},... | collective-permute-start | bytes 1572872 | tf_op jit(solution)/shard_map/ppermute | solution.py:14
  831.5 17.6 %collective-permute-start.54 = (f32[2,256,256]{2,1,0:T(8,128)S(1)}, f32[2,256,256]{2,1,0:T(8,128)S(1)}, u32[]{:S(2)}, u32[]{:S(2)}) collective-permute-start(f32[2,256,256]{2,1,0:T(8,128)S(1)} %get-tuple-element.16), channel_id=1, source_target_pairs={{0,16},{4,20},{8,24},{12,28},{16,0},{20,4},{24,8},{28,12},{32,48},... | collective-permute-start | bytes 1572872 | tf_op jit(solution)/shard_map/ppermute | solution.py:14
  851.4 20.1 %collective-permute-start.56 = (f32[2,256,256]{2,1,0:T(8,128)S(1)}, f32[2,256,256]{2,1,0:T(8,128)S(1)}, u32[]{:S(2)}, u32[]{:S(2)}) collective-permute-start(f32[2,256,256]{2,1,0:T(8,128)S(1)} %get-tuple-element.14), channel_id=1, source_target_pairs={{0,32},{4,36},{8,40},{12,44},{16,48},{20,52},{24,56},{28,60},{32,0... | collective-permute-start | bytes 1572872 | tf_op jit(solution)/shard_map/ppermute | solution.py:14
  872.7 31.7 %collective-permute-start.57 = (f32[2,256,256]{2,1,0:T(8,128)}, f32[2,256,256]{2,1,0:T(8,128)}, u32[]{:S(2)}, u32[]{:S(2)}) collective-permute-start(f32[2,256,256]{2,1,0:T(8,128)} %get-tuple-element.13), channel_id=1, source_target_pairs={{0,64},{4,68},{8,72},{12,76},{16,80},{20,84},{24,88},{28,92},{32,9... | collective-permute-start | bytes 1572872 | tf_op jit(solution)/shard_map/ppermute | solution.py:14
  872.7 43.0 %collective-permute-start.58 = (f32[2,256,256]{2,1,0:T(8,128)S(1)}, f32[2,256,256]{2,1,0:T(8,128)}, u32[]{:S(2)}, u32[]{:S(2)}) collective-permute-start(f32[2,256,256]{2,1,0:T(8,128)S(1)} %get-tuple-element.12), channel_id=1, source_target_pairs={{0,64},{4,68},{8,72},{12,76},{16,80},{20,84},{24,88},{28,92},{32,9... | collective-permute-start | bytes 1572872 | tf_op jit(solution)/shard_map/ppermute | solution.py:14
  876.4 131.9 %reduce-scatter.5.cloned.1.call-start = ((), (), s32[]{:S(2)}) async-start(), calls=%async_computation.3 | async-start | bytes 1310720 | tf_op jit(solution)/shard_map/reduce_scatter | solution.py:199
  917.4 43.9 %collective-permute-start.59 = (f32[2,256,256]{2,1,0:T(8,128)S(1)}, f32[2,256,256]{2,1,0:T(8,128)S(1)}, u32[]{:S(2)}, u32[]{:S(2)}) collective-permute-start(f32[2,256,256]{2,1,0:T(8,128)S(1)} %get-tuple-element.11), channel_id=1, source_target_pairs={{0,128},{4,132},{8,136},{12,140},{16,144},{20,148},{24,152},{28,15... | collective-permute-start | bytes 1572872 | tf_op jit(solution)/shard_map/ppermute | solution.py:14
  921.6 51.0 %collective-permute-start.60 = (f32[2,256,256]{2,1,0:T(8,128)S(1)}, f32[2,256,256]{2,1,0:T(8,128)S(1)}, u32[]{:S(2)}, u32[]{:S(2)}) collective-permute-start(f32[2,256,256]{2,1,0:T(8,128)S(1)} %get-tuple-element.10), channel_id=1, source_target_pairs={{0,128},{4,132},{8,136},{12,140},{16,144},{20,148},{24,152},{28,15... | collective-permute-start | bytes 1572872 | tf_op jit(solution)/shard_map/ppermute | solution.py:14
  (40 other events, 650.2 us)
Sparse Core Ops, SparseCore 0:
  876.5 54.8 reduce-scatter.2
  981.8 26.4 reduce-scatter.4
where the time goes:
time: 1030 us; the launch traced here: 1020 us
  waiting for transfers between devices  660 us (64%)
  starting transfers between devices  192 us (19%)
  blocking collectives  54.9 us (5%)
  other arithmetic  45.7 us (4%)
  matrix products  41.5 us (4%)
  between operations  16.8 us (2%)
    ppermute x60, waiting for transfers between devices, partner(): return lax.ppermute(value, axis, pairs)  630 us
    ppermute x60, starting transfers between devices, partner(): return lax.ppermute(value, axis, pairs)  188 us
    all_gather x1, blocking collectives, local(): lax.all_gather(cotangent, 'panel', axis=1, tiled=True)  45 us
    reduce_scatter x1, waiting for transfers between devices, local(): lax.psum_scatter(grad_partial, 'panel', scatter_dimension=1, tiled=True)  25 us
    select_n x18, other arithmetic, across_forward(): real_part = jnp.where(upper_side, diff_real, real_part + partner_real)  21.2 us
  transfers between devices with their start and end apart: 64, of which 55 were waited for; matrix products, arithmetic and copies ran while one was open for 4% of the time, Pallas kernels for 0%

commit v1 on v0

v1 whole, which is shorter than its diff:
```python
import jax
import jax.numpy as jnp
from jax import lax
from jax.experimental import pallas as pl
from jax.experimental.pallas import tpu as pltpu
from jax.sharding import PartitionSpec as P

F32, BF16 = jnp.float32, jnp.bfloat16


def conv_kernel(x_ref, h_ref, y_ref, r_ref):
    row = lax.broadcasted_iota(jnp.int32, (128, 128), 0)
    col = lax.broadcasted_iota(jnp.int32, (128, 128), 1)
    keep = col >= row
    r_ref[128:256, 0:128] = jnp.zeros((128, 128), BF16)

    def build(k, prev):
        u = jnp.broadcast_to(h_ref[0, pl.ds(k, 1), :], (128, 128))
        v = pltpu.roll(u, 0, 1, stride=1, stride_axis=0)
        m = jnp.where(keep, v, prev).astype(BF16)
        at = pl.multiple_of(k * 128, 128)
        r_ref[0:128, pl.ds(at, 128)] = m
        r_ref[128:256, pl.ds(at + 128, 128)] = m
        return v

    lax.fori_loop(0, 128, build, jnp.zeros((128, 128), F32))

    sub = lax.broadcasted_iota(jnp.int32, (8, 2, 8, 256), 2)
    total = jnp.zeros((8, 2, 8, 256), F32)
    for r in range(8):
        z = jnp.dot(
            x_ref[0], r_ref[:, r * 256 : (r + 1) * 256], preferred_element_type=F32
        )
        for q in range(1, 8):
            at = (8 * q + r) * 256
            part = jnp.dot(
                x_ref[0, 0 : 128 - 16 * q, :],
                r_ref[:, at : at + 256],
                preferred_element_type=F32,
            )
            z = jnp.concatenate([z[: 16 * q], z[16 * q :] + part], axis=0)
        if r == 0:
            total = total + z.reshape(8, 2, 8, 256)
        else:
            turned = pltpu.roll(z.reshape(16, 8, 256), r, 1).reshape(8, 2, 8, 256)
            before = jnp.concatenate(
                [jnp.zeros((1, 2, 8, 256), F32), turned[:-1]], axis=0
            )
            total = total + jnp.where(sub >= r, turned, before)
    y_ref[0] = total.reshape(128, 256).astype(BF16)


def conv(x, h):
    return pl.pallas_call(
        conv_kernel,
        grid=(4,),
        out_shape=jax.ShapeDtypeStruct((4, 128, 256), BF16),
        in_specs=[
            pl.BlockSpec((1, 128, 256), lambda c: (c, 0, 0)),
            pl.BlockSpec((1, 128, 128), lambda c: (c, 0, 0)),
        ],
        out_specs=pl.BlockSpec((1, 128, 256), lambda c: (c, 0, 0)),
        scratch_shapes=[pltpu.VMEM((256, 16384 + 128), BF16)],
        compiler_params=pltpu.CompilerParams(vmem_limit_bytes=32 * 2**20),
    )(x, h)


def shifted(value, axis, steps):
    count = lax.axis_size(axis)
    initial, last = (max(0, -steps), min(count, count - steps))
    return lax.ppermute(value, axis, [(source, source + steps) for source in range(initial, last)])


def local(tokens, cotangent, in_weight, short_kernel, skip_gain, long_filter, out_weight):
    row_count = tokens.shape[0]
    tap_count = short_kernel.shape[0]
    n = lax.axis_size("seq")
    h = lax.all_to_all(
        long_filter.astype(BF16).T.reshape(n, 4, row_count), "seq", 0, 0
    )
    h = h.transpose(1, 0, 2).reshape(4, 128, 128).astype(F32)
    full_tok, full_cot = (
        lax.all_gather(tokens, "panel", axis=1, tiled=True),
        lax.all_gather(cotangent, "panel", axis=1, tiled=True),
    )
    projected = jnp.einsum(
        "td,jdc->jtc", full_tok, in_weight, preferred_element_type=F32
    ).astype(BF16)
    before = shifted(projected[:, row_count - (tap_count - 1) :, :], "seq", 1)
    extended = jnp.concatenate([before, projected], axis=1).astype(F32)
    filtered = short_kernel[0][:, None, :] * extended[:, tap_count - 1 :, :]
    for tap_index in range(1, tap_count):
        filtered = (
            filtered
            + short_kernel[tap_index][:, None, :]
            * extended[:, tap_count - 1 - tap_index : tap_count - 1 - tap_index + row_count, :]
        )
    gate_out, gate_in, value_path = (filtered[0], filtered[1], filtered[2])
    signal = value_path * gate_in
    grad_gated = lax.dot_general(
        full_cot, out_weight, (((1,), (1,)), ((), ())), preferred_element_type=F32
    )
    grad_state = grad_gated * gate_out

    both = jnp.stack([signal.T, grad_state[::-1].T], axis=1).astype(BF16)
    both = lax.all_to_all(both.reshape(n, 4, 2, row_count), "seq", 0, 0)
    xs = both[:, :, 0].transpose(1, 0, 2).reshape(4, 8, 1, 8, row_count)
    xg = both[::-1, :, 1].transpose(1, 0, 2).reshape(4, 8, 1, 8, row_count)
    x = jnp.concatenate([xs, xg], axis=2).reshape(4, 128, row_count)
    y = conv(x, h).reshape(4, 8, 2, 8, row_count)
    ys = y[:, :, 0].reshape(4, n, row_count).transpose(1, 0, 2)
    yg = y[:, :, 1].reshape(4, n, row_count).transpose(1, 0, 2)[::-1]
    back = lax.all_to_all(jnp.stack([ys, yg], axis=2), "seq", 0, 0).reshape(256, 2, row_count)
    conv_state = back[:, 0].T.astype(F32) + skip_gain[None, :] * signal
    grad_signal = back[:, 1].T[::-1].astype(F32) + skip_gain[None, :] * grad_state

    gated_state = (conv_state * gate_out).astype(BF16)
    partial_value = jnp.dot(gated_state, out_weight, preferred_element_type=F32)
    block_out = lax.psum_scatter(partial_value, "panel", scatter_dimension=1, tiled=True).astype(
        BF16
    )
    grad_gate_out = grad_gated * conv_state
    grad_value = grad_signal * gate_in
    grad_gate_in = grad_signal * value_path
    upstream = jnp.stack([grad_gate_out, grad_gate_in, grad_value])
    after_rim = shifted(upstream[:, : tap_count - 1, :], "seq", -1)
    widened = jnp.concatenate([upstream, after_rim], axis=1)
    grad_projected = short_kernel[0][:, None, :] * widened[:, :row_count, :]
    for tap_index in range(1, tap_count):
        grad_projected = (
            grad_projected
            + short_kernel[tap_index][:, None, :] * widened[:, tap_index : tap_index + row_count, :]
        )
    grad_projected = grad_projected.astype(BF16)
    grad_partial = jnp.einsum("jtc,jdc->td", grad_projected, in_weight, preferred_element_type=F32)
    token_grad = lax.psum_scatter(grad_partial, "panel", scatter_dimension=1, tiled=True).astype(
        BF16
    )
    return (block_out, token_grad)


def solution(mesh):
    placed = (
        P("seq", "panel"),
        P("seq", "panel"),
        P(None, None, "panel"),
        P(None, None, "panel"),
        P("panel"),
        P("seq", "panel"),
        P("panel", None),
    )
    return jax.shard_map(
        local,
        mesh=mesh,
        in_specs=placed,
        out_specs=(P("seq", "panel"), P("seq", "panel")),
        check_vma=False,
    )
```

time: 1030 us -> 202 us (0.20); the launches traced: 1020 us -> 201 us
  waiting for transfers between devices: 660 us -> 48.7 us
  starting transfers between devices: 192 us -> 31 us
  Pallas kernels: 0 us -> 51.6 us
  other arithmetic: 45.7 us -> 6.19 us
  matrix products: 41.5 us -> 3.85 us
  blocking collectives: 54.9 us -> 36.4 us
    ppermute x60 -> x0, waiting for transfers between devices: 630 us -> none  [partner(): return lax.ppermute(value, axis, pairs)]
    ppermute x60 -> x0, starting transfers between devices: 188 us -> none  [partner(): return lax.ppermute(value, axis, pairs)]
    pallas_call x0 -> x1, Pallas kernels: none -> 51.6 us  [conv(): pl.pallas_call(conv_kernel, grid=(4,), out_shape=jax.ShapeDtypeStruct((4,...]
    select_n x30 -> x0, other arithmetic: 38.8 us -> none  [the longest x18 21.2 us: across_forward(): real_part = jnp.where(upper_side, diff_real, real_part + partner_real)]
    all_gather x1, blocking collectives: 45 us -> 7.31 us  [local(): lax.all_gather(cotangent, 'panel', axis=1, tiled=True)]
    dot_general x22 -> x2, matrix products: 38.3 us -> 1.86 us  [the longest x1 1.29 us: local(): partial_value = jnp.dot(gated_state, out_weight, preferred_element_type=F32)]
    all_to_all x0 -> x2, starting transfers between devices: none -> 26.4 us  [the longest x1 15.1 us: local(): lax.all_to_all(long_filter.astype(BF16).T.reshape(n, 4, row_count), 'seq'...]
    all_to_all x0 -> x1, blocking collectives: none -> 20.2 us  [local(): lax.all_to_all(jnp.stack([ys, yg], axis=2), 'seq', 0, 0)]
  transfers between devices with their start and end apart: 64 -> 6, of which waited for: 55 -> 4; matrix products, arithmetic and copies ran while one was open for 4% -> 5% of each run, Pallas kernels for 0% -> 0%
where the time goes in v1:
time: 202 us; the launch traced here: 201 us
  Pallas kernels  51.6 us (26%)
  waiting for transfers between devices  48.7 us (24%)
  blocking collectives  36.4 us (18%)
  starting transfers between devices  31 us (15%)
  between operations  14.3 us (7%)
  local copies, waits for them, and re-layouts  9.14 us (5%)
  other arithmetic  6.19 us (3%)
  matrix products  3.85 us (2%)
    pallas_call x1, Pallas kernels, conv(): pl.pallas_call(conv_kernel, grid=(4,), out_shape=jax.ShapeDtypeStruct((4,...  51.6 us
    reduce_scatter x1, waiting for transfers between devices, local(): lax.psum_scatter(grad_partial, 'panel', scatter_dimension=1, tiled=True)  24.4 us
    all_to_all x1, blocking collectives, local(): lax.all_to_all(jnp.stack([ys, yg], axis=2), 'seq', 0, 0)  20.2 us
    all_to_all x1, starting transfers between devices, local(): lax.all_to_all(long_filter.astype(BF16).T.reshape(n, 4, row_count), 'seq'...  15.1 us
    all_to_all x1, starting transfers between devices, local(): both = lax.all_to_all(both.reshape(n, 4, 2, row_count), 'seq', 0, 0)  11.3 us
    all_to_all x1, waiting for transfers between devices, local(): both = lax.all_to_all(both.reshape(n, 4, 2, row_count), 'seq', 0, 0)  11.2 us
    reduce_scatter x1, waiting for transfers between devices, local(): lax.psum_scatter(partial_value, 'panel', scatter_dimension=1, tiled=True)  10 us
    all_gather x1, blocking collectives, local(): lax.all_gather(tokens, 'panel', axis=1, tiled=True)  8.84 us
  transfers between devices with their start and end apart: 6, of which 4 were waited for; matrix products, arithmetic and copies ran while one was open for 5% of the time, Pallas kernels for 0%

profile of v1, /device:TPU:1, one launch (start us, length us, event | category | flops | bytes accessed | tf_op | source)
XLA Modules:
  0.0 201.1 jit_solution(4647286968488626617)
XLA Ops:
  7.2 0.0 copy-start
  7.2 1.1 convert_bitcast_fusion.2
  8.3 0.1 copy.38
  8.4 0.7 reshape.41
  9.1 15.1 %all-to-all-start.1 = ((bf16[64,4,256]{2,1,0:T(4,128)(2,1)}), bf16[64,4,256]{2,1,0:T(4,128)(2,1)S(1)}, u32[]{:S(2)}, u32[]{:S(2)}) async-start(bf16[64,4,256]{2,1,0:T(4,128)(2,1)} %reshape.41), calls=%async_computation.1 | async-start | bytes 262144 | tf_op jit(solution)/shard_map/all_to_all | solution.py:78
  24.2 8.8 %all_gather.6 = bf16[256,1024]{1,0:T(8,128)(2,1)S(1)} all-gather(bf16[256,256]{1,0:T(8,128)(2,1)} %param.7), channel_id=1, replica_groups=mesh['seq'=64,'panel'=4] {'panel'}, dimensions={1}, use_global_device_ids=true | all-gather | bytes 655360 | tf_op jit(solution)/shard_map/all_gather | solution.py:83
  33.0 0.6 fusion
  33.6 3.3 %collective-permute-start = (bf16[3,2,256]{2,1,0:T(2,128)(2,1)S(1)}, bf16[3,2,256]{2,1,0:T(2,128)(2,1)S(1)}, u32[]{:S(2)}, u32[]{:S(2)}) collective-permute-start(bf16[3,2,256]{2,1,0:T(2,128)(2,1)S(1)} %slice.79), channel_id=1, source_target_pairs={{0,4},{4,8},{8,12},{12,16},{16,20},{20,24},{24,28},{28,32},{32,36}... | collective-permute-start | bytes 9224 | tf_op jit(solution)/shard_map/ppermute | solution.py:71
  36.9 7.3 %all_gather.7 = bf16[256,1024]{1,0:T(8,128)(2,1)S(1)} all-gather(bf16[256,256]{1,0:T(8,128)(2,1)S(1)} %copy-done.3), channel_id=1, replica_groups=mesh['seq'=64,'panel'=4] {'panel'}, dimensions={1}, use_global_device_ids=true | all-gather | bytes 655360 | tf_op jit(solution)/shard_map/all_gather | solution.py:84
  44.2 0.3 fusion.20
  44.6 0.1 maximum_convert_fusion
  44.7 0.2 fusion.4
  44.9 0.1 convert_bitcast_fusion.4
  45.0 0.1 copy.33
  45.2 0.2 rev.12
  45.3 0.1 copy.34
  45.5 0.2 pad_maximum_fusion.2
  45.7 0.8 copy.35
  46.5 11.3 %all-to-all-start = ((bf16[64,4,2,256]{3,1,2,0:T(4,128)(2,1)}), bf16[64,4,2,256]{3,1,2,0:T(4,128)(2,1)S(1)}, u32[]{:S(2)}, u32[]{:S(2)}) async-start(bf16[64,4,2,256]{3,1,2,0:T(4,128)(2,1)} %copy.35), calls=%async_computation | async-start | bytes 524288 | tf_op jit(solution)/shard_map/all_to_all | solution.py:106
  57.7 0.0 reduce-scatter.3.cloned.1.call-start
  57.8 0.7 copy.39
  58.6 1.0 reshape.44.h_ref
  59.5 11.2 %all-to-all-done = bf16[64,4,2,256]{3,1,2,0:T(4,128)(2,1)S(1)} async-done(((bf16[64,4,2,256]{3,1,2,0:T(4,128)(2,1)}), bf16[64,4,2,256]{3,1,2,0:T(4,128)(2,1)S(1)}, u32[]{:S(2)}, u32[]{:S(2)}) %all-to-all-start) | async-done | bytes 262176 | tf_op jit(solution)/shard_map/all_to_all | solution.py:106
  70.7 0.1 fusion.19
  70.9 51.6 %shard_map.86 = bf16[4,128,256]{2,1,0:T(8,128)(2,1)S(1)} custom-call(bf16[4,128,256]{2,1,0:T(8,128)(2,1)S(1)} %bitcast.110, f32[4,128,128]{2,1,0:T(8,128)S(1)} %reshape.44.h_ref), custom_call_target="tpu_custom_call" | custom-call | tf_op jit(solution)/shard_map/pallas_call | solution.py:54
  122.5 0.7 slice_bitcast_fusion.4
  123.2 0.7 rev.14
  123.9 1.1 pad_maximum_fusion.4
  125.0 0.3 copy.40
  125.2 20.2 %all_to_all.15 = bf16[64,4,2,256]{3,2,1,0:T(2,128)(2,1)S(1)} all-to-all(bf16[64,4,2,256]{3,2,1,0:T(2,128)(2,1)S(1)} %copy.40), channel_id=1, replica_groups=mesh['seq'=64,'panel'=4] {'seq'}, dimensions={0} | all-to-all | bytes 524288 | tf_op jit(solution)/shard_map/all_to_all | solution.py:113
  145.5 1.2 fusion.18
  146.7 1.1 copy.43
  147.8 1.3 fusion.14
  149.0 0.0 reduce-scatter.3.cloned.1.call-update
  149.1 0.0 reduce-scatter.5.cloned.1.call-start
  149.1 1.1 copy.44
  150.2 0.2 rev.15
  150.4 0.1 multiply_bitcast_fusion.1
  150.5 0.1 pad_maximum_fusion.1
  150.6 1.3 collective-permute-start.1
  151.9 3.1 %collective-permute-done.1 = f32[3,2,256]{2,1,0:T(2,128)S(1)} collective-permute-done((f32[3,2,256]{2,1,0:T(2,128)S(1)}, f32[3,2,256]{2,1,0:T(2,128)S(1)}, u32[]{:S(2)}, u32[]{:S(2)}) %collective-permute-start.1) | collective-permute-done | bytes 6176 | tf_op jit(solution)/shard_map/ppermute | solution.py:71
  154.9 0.1 pad_maximum_fusion
  155.0 1.7 convolution_bitcast_fusion
  156.7 0.0 reduce-scatter.5.cloned.1.call-update
  156.7 10.0 %reduce-scatter.3.cloned.1.call-done = f32[256,256]{1,0:T(8,128)} async-done(((f32[256,1024]{1,0:T(8,128)}), f32[256,256]{1,0:T(8,128)}) %reduce-scatter.3.cloned.1.call-update) | async-done | bytes 262160 | tf_op jit(solution)/shard_map/reduce_scatter | solution.py:119
  166.7 1.6 convert_element_type.56
  168.3 24.4 %reduce-scatter.5.cloned.1.call-done = f32[256,256]{1,0:T(8,128)} async-done(((f32[256,1024]{1,0:T(8,128)}), f32[256,256]{1,0:T(8,128)}) %reduce-scatter.5.cloned.1.call-update) | async-done | bytes 262160 | tf_op jit(solution)/shard_map/reduce_scatter | solution.py:136
  192.7 1.6 convert_element_type.59
  (23 shorter events, 0.3 us)
Async XLA Ops:
  7.2 25.9 %copy-start = (bf16[3,1024,256]{2,1,0:T(8,128)(2,1)S(1)}, bf16[3,1024,256]{2,1,0:T(8,128)(2,1)}, u32[]{:S(2)}) copy-start(bf16[3,1024,256]{2,1,0:T(8,128)(2,1)} %param.9) | copy-start | bytes 4718596
  9.1 37.4 %all-to-all-start.1 = ((bf16[64,4,256]{2,1,0:T(4,128)(2,1)}), bf16[64,4,256]{2,1,0:T(4,128)(2,1)S(1)}, u32[]{:S(2)}, u32[]{:S(2)}) async-start(bf16[64,4,256]{2,1,0:T(4,128)(2,1)} %reshape.41), calls=%async_computation.1 | async-start | bytes 262144 | tf_op jit(solution)/shard_map/all_to_all | solution.py:78
  24.2 12.7 %copy-start.3 = (bf16[256,256]{1,0:T(8,128)(2,1)S(1)}, bf16[256,256]{1,0:T(8,128)(2,1)}, u32[]{:S(2)}) copy-start(bf16[256,256]{1,0:T(8,128)(2,1)} %param.8) | copy-start | bytes 393220
  33.0 11.2 %copy-start.1 = (bf16[256,1024]{1,0:T(8,128)(2,1)S(1)}, bf16[256,1024]{1,0:T(8,128)(2,1)}, u32[]{:S(2)}) copy-start(bf16[256,1024]{1,0:T(8,128)(2,1)} %param.13) | copy-start | bytes 1572868
  33.6 11.0 %copy-start.4 = (f32[3,3,256]{2,1,0:T(4,128)S(1)}, f32[3,3,256]{2,1,0:T(4,128)}, u32[]{:S(2)}) copy-start(f32[3,3,256]{2,1,0:T(4,128)} %param.10) | copy-start | bytes 27652
  33.6 11.0 %collective-permute-start = (bf16[3,2,256]{2,1,0:T(2,128)(2,1)S(1)}, bf16[3,2,256]{2,1,0:T(2,128)(2,1)S(1)}, u32[]{:S(2)}, u32[]{:S(2)}) collective-permute-start(bf16[3,2,256]{2,1,0:T(2,128)(2,1)S(1)} %slice.79), channel_id=1, source_target_pairs={{0,4},{4,8},{8,12},{12,16},{16,20},{20,24},{24,28},{28,32},{32,36}... | collective-permute-start | bytes 9224 | tf_op jit(solution)/shard_map/ppermute | solution.py:71
  46.5 24.2 %all-to-all-start = ((bf16[64,4,2,256]{3,1,2,0:T(4,128)(2,1)}), bf16[64,4,2,256]{3,1,2,0:T(4,128)(2,1)S(1)}, u32[]{:S(2)}, u32[]{:S(2)}) async-start(bf16[64,4,2,256]{3,1,2,0:T(4,128)(2,1)} %copy.35), calls=%async_computation | async-start | bytes 524288 | tf_op jit(solution)/shard_map/all_to_all | solution.py:106
  57.7 108.9 %reduce-scatter.3.cloned.1.call-start = ((), (), s32[]{:S(2)}) async-start(), calls=%async_computation.5 | async-start | bytes 1310720 | tf_op jit(solution)/shard_map/reduce_scatter | solution.py:119
  123.9 23.8 %copy-start.2 = (bf16[256,1024]{1,0:T(8,128)(2,1)S(1)}, bf16[256,1024]{1,0:T(8,128)(2,1)}, u32[]{:S(2)}) copy-start(bf16[256,1024]{1,0:T(8,128)(2,1)} %param.13) | copy-start | bytes 1572868
  123.9 23.9 %copy-start.5 = (f32[256]{0:T(256)S(1)}, f32[256]{0:T(256)}, u32[]{:S(2)}) copy-start(f32[256]{0:T(256)} %param.11) | copy-start | bytes 3076
  149.1 43.6 %reduce-scatter.5.cloned.1.call-start = ((), (), s32[]{:S(2)}) async-start(), calls=%async_computation.6 | async-start | bytes 1310720 | tf_op jit(solution)/shard_map/reduce_scatter | solution.py:136
  150.6 4.4 %collective-permute-start.1 = (f32[3,2,256]{2,1,0:T(2,128)S(1)}, f32[3,2,256]{2,1,0:T(2,128)S(1)}, u32[]{:S(2)}, u32[]{:S(2)}) collective-permute-start(f32[3,2,256]{2,1,0:T(2,128)S(1)} %slice.92), channel_id=1, source_target_pairs={{4,0},{8,4},{12,8},{16,12},{20,16},{24,20},{28,24},{32,28},{36,32}... | collective-permute-start | bytes 18440 | tf_op jit(solution)/shard_map/ppermute | solution.py:71
Sparse Core Ops, SparseCore 0:
  149.2 17.4 reduce-scatter.2
  169.4 23.2 reduce-scatter.4

commit v2 on v1

v2 whole, which is shorter than its diff:
```python
import functools

import jax
import jax.numpy as jnp
from jax import lax
from jax.experimental import pallas as pl
from jax.experimental.pallas import tpu as pltpu
from jax.sharding import PartitionSpec as P

F32, BF16 = jnp.float32, jnp.bfloat16


MESH = pl.DeviceIdType.MESH


def identity(flip):
    row = lax.broadcasted_iota(jnp.int32, (256, 256), 0)
    col = lax.broadcasted_iota(jnp.int32, (256, 256), 1)
    return jnp.where(row + col == 255 if flip else row == col, 1.0, 0.0).astype(BF16)


def turn(select, value):
    return lax.dot_general(select, value, (((1,), (1,)), ((), ())), preferred_element_type=F32)


def interleave(first, second):
    first, second = first.reshape(32, 8, 128), second.reshape(32, 8, 128)
    upper = lax.broadcasted_iota(jnp.int32, (32, 8, 128), 1) < 4
    even = jnp.where(upper, first, pltpu.roll(second, 4, 1))
    odd = jnp.where(upper, pltpu.roll(first, 4, 1), second)
    return even, odd


def exchange(n, send_ref, recv_ref, offset, sems):
    me = lax.axis_index("seq")

    def one(j, carry):
        to = lax.rem(me + j, n)
        pltpu.make_async_remote_copy(
            src_ref=send_ref.at[to],
            dst_ref=recv_ref.at[me + offset],
            send_sem=sems.at[0],
            recv_sem=sems.at[1],
            device_id={"seq": to},
            device_id_type=MESH,
        ).start()
        return carry

    lax.fori_loop(1, n, one, 0)
    recv_ref[me + offset] = send_ref[me]


def await_all(n, ref, sem):
    part = ref.at[pl.ds(0, n - 1)]
    pltpu.make_async_copy(part, part, sem).wait()


def build_toeplitz(hr, r_ref):
    row = lax.broadcasted_iota(jnp.int32, (128, 128), 0)
    col = lax.broadcasted_iota(jnp.int32, (128, 128), 1)
    cut = col >= 128 - row

    def channel(c, carry):
        r_ref[c, 128:256, 0:128] = jnp.zeros((128, 128), BF16)

        def block(a, carry):
            early = jnp.broadcast_to(hr[a, pl.ds(c + 4, 1), :], (128, 128))
            for half in range(2):
                now = jnp.broadcast_to(hr[a + 1, pl.ds(c + 4 * half, 1), :], (128, 128))
                mixed = jnp.where(cut, early, now)
                tile = pltpu.roll(mixed, 0, 1, stride=1, stride_axis=0).astype(BF16)
                at = pl.multiple_of(a * 256, 256) + 128 * half
                r_ref[c, 0:128, pl.ds(at, 128)] = tile
                r_ref[c, 128:256, pl.ds(at + 128, 128)] = tile
                early = now
            return carry

        lax.fori_loop(0, 64, block, 0, unroll=8)
        return carry

    lax.fori_loop(0, 4, channel, 0)


def convolve(xr, xf, xl, tot, r_ref, yf, ys):
    xf[...] = xr[...].astype(F32).reshape(1024, 128)
    for c in range(4):
        rows = []
        for j in range(8):
            s_at, g_at = 128 * j + c, 128 * (7 - j) + 4 + c
            for at in (s_at, g_at):
                rows.append(
                    jnp.concatenate(
                        [xf[pl.ds(at, 8, stride=16), :], xf[pl.ds(at + 8, 8, stride=16), :]], axis=1
                    )
                )
        x = jnp.concatenate(rows, axis=0).astype(BF16)
        xl[c, :, 0:256] = x
        for q in range(1, 8):
            xl[c, 0 : 16 * q, 256 * q : 256 * (q + 1)] = jnp.zeros((16 * q, 256), BF16)
            xl[c, 16 * q :, 256 * q : 256 * (q + 1)] = x[: 128 - 16 * q]

    sub = lax.broadcasted_iota(jnp.int32, (8, 8, 256), 1)

    def channel(c, carry):
        total = [None, None]
        for r in range(8):
            z = None
            for q in range(8):
                at = (8 * q + r) * 256
                part = jnp.dot(
                    xl[c, :, 256 * q : 256 * (q + 1)],
                    r_ref[c, :, at : at + 256],
                    preferred_element_type=F32,
                )
                z = part if z is None else z + part
            z = z.reshape(8, 2, 8, 256)
            for side in range(2):
                zs = z[:, side]
                if r == 0:
                    total[side] = zs
                    continue
                turned = pltpu.roll(zs, r if side == 0 else 8 - r, 1)
                before = jnp.concatenate([jnp.zeros((1, 8, 256), F32), turned[:-1]], axis=0)
                inside = sub >= r if side == 0 else sub < 8 - r
                total[side] = total[side] + jnp.where(inside, turned, before)
        for side in range(2):
            tot[c, side] = total[side]
        return carry

    lax.fori_loop(0, 4, channel, 0)
    for c in range(4):
        for j in range(8):
            s_at, g_at = 128 * j + c, 128 * (7 - j) + 4 + c
            for side, at in ((0, s_at), (1, g_at)):
                yf[pl.ds(at, 8, stride=16), :] = tot[c, side, j, :, 0:128]
                yf[pl.ds(at + 8, 8, stride=16), :] = tot[c, side, j, :, 128:256]
    ys[...] = yf[...].reshape(64, 16, 128).astype(BF16)


def conv_kernel(
    n, s_ref, g_ref, f_ref, so_ref, go_ref, hs, hr, xs, xr, xf, xl, tot, r_ref, yf, ys, yr, hsem, xsem, ysem
):
    me = lax.axis_index("seq")
    barrier = pltpu.get_barrier_semaphore()

    def greet(j, carry):
        pl.semaphore_signal(
            barrier, inc=1, device_id={"seq": lax.rem(me + j, n)}, device_id_type=MESH
        )
        return carry

    lax.fori_loop(1, n, greet, 0)
    eye, flip = identity(False), identity(True)
    ft = turn(eye, f_ref[...].astype(BF16))
    even, odd = interleave(ft[:, :128], ft[:, 128:])
    hs[...] = jnp.stack([even, odd], axis=1).reshape(64, 8, 128)
    hr[0] = jnp.zeros((8, 128), F32)
    pl.semaphore_wait(barrier, n - 1)
    exchange(n, hs, hr, 1, hsem)

    st = turn(eye, s_ref[...].astype(BF16))
    gf = jnp.dot(flip, g_ref[...].astype(BF16), preferred_element_type=F32)
    gt = turn(eye, gf.astype(BF16))
    even_lo, odd_lo = interleave(st[:, :128], gt[:, :128])
    even_hi, odd_hi = interleave(st[:, 128:], gt[:, 128:])
    even = jnp.concatenate([even_lo, even_hi], axis=1)
    odd = jnp.concatenate([odd_lo, odd_hi], axis=1)
    xs[...] = jnp.stack([even, odd], axis=1).reshape(64, 16, 128).astype(BF16)
    exchange(n, xs, xr, 0, xsem)

    await_all(n, hr, hsem.at[1])
    build_toeplitz(hr, r_ref)
    await_all(n, xr, xsem.at[1])
    convolve(xr, xf, xl, tot, r_ref, yf, ys)
    exchange(n, ys, yr, 0, ysem)
    await_all(n, yr, ysem.at[1])

    back = yr[...].astype(F32).reshape(32, 2, 16, 128)
    upper = lax.broadcasted_iota(jnp.int32, (32, 8, 128), 1) < 4
    cols_s, cols_g = [], []
    for half in range(2):
        even = back[:, 0, 8 * half : 8 * half + 8]
        odd = back[:, 1, 8 * half : 8 * half + 8]
        cols_s.append(jnp.where(upper, even, pltpu.roll(odd, 4, 1)).reshape(256, 128))
        cols_g.append(jnp.where(upper, pltpu.roll(even, 4, 1), odd).reshape(256, 128))
    so_ref[...] = turn(eye, jnp.concatenate(cols_s, axis=1).astype(BF16))
    go_ref[...] = turn(flip, jnp.concatenate(cols_g, axis=1).astype(BF16))
    await_all(n, hr, hsem.at[0])
    await_all(n, xr, xsem.at[0])
    await_all(n, yr, ysem.at[0])


def conv(signal, grad_state, long_filter):
    n = lax.axis_size("seq")
    out = jax.ShapeDtypeStruct((256, 256), F32)
    vmem = pl.BlockSpec(memory_space=pltpu.VMEM)
    return pl.pallas_call(
        functools.partial(conv_kernel, n),
        out_shape=(out, out),
        in_specs=[vmem] * 3,
        out_specs=(vmem, vmem),
        scratch_shapes=[
            pltpu.VMEM((64, 8, 128), F32),
            pltpu.VMEM((65, 8, 128), F32),
            pltpu.VMEM((64, 16, 128), BF16),
            pltpu.VMEM((64, 16, 128), BF16),
            pltpu.VMEM((1024, 128), F32),
            pltpu.VMEM((4, 128, 2048), BF16),
            pltpu.VMEM((4, 2, 8, 8, 256), F32),
            pltpu.VMEM((4, 256, 16384 + 128), BF16),
            pltpu.VMEM((1024, 128), F32),
            pltpu.VMEM((64, 16, 128), BF16),
            pltpu.VMEM((64, 16, 128), BF16),
            pltpu.SemaphoreType.DMA((2,)),
            pltpu.SemaphoreType.DMA((2,)),
            pltpu.SemaphoreType.DMA((2,)),
        ],
        compiler_params=pltpu.CompilerParams(
            collective_id=0, has_side_effects=True, vmem_limit_bytes=56 * 2**20
        ),
    )(signal, grad_state, long_filter)


def shifted(value, axis, steps):
    count = lax.axis_size(axis)
    initial, last = (max(0, -steps), min(count, count - steps))
    return lax.ppermute(value, axis, [(source, source + steps) for source in range(initial, last)])


def local(tokens, cotangent, in_weight, short_kernel, skip_gain, long_filter, out_weight):
    row_count = tokens.shape[0]
    tap_count = short_kernel.shape[0]
    full_tok, full_cot = (
        lax.all_gather(tokens, "panel", axis=1, tiled=True),
        lax.all_gather(cotangent, "panel", axis=1, tiled=True),
    )
    projected = jnp.einsum(
        "td,jdc->jtc", full_tok, in_weight, preferred_element_type=F32
    ).astype(BF16)
    before = shifted(projected[:, row_count - (tap_count - 1) :, :], "seq", 1)
    extended = jnp.concatenate([before, projected], axis=1).astype(F32)
    filtered = short_kernel[0][:, None, :] * extended[:, tap_count - 1 :, :]
    for tap_index in range(1, tap_count):
        filtered = (
            filtered
            + short_kernel[tap_index][:, None, :]
            * extended[:, tap_count - 1 - tap_index : tap_count - 1 - tap_index + row_count, :]
        )
    gate_out, gate_in, value_path = (filtered[0], filtered[1], filtered[2])
    signal = value_path * gate_in
    grad_gated = lax.dot_general(
        full_cot, out_weight, (((1,), (1,)), ((), ())), preferred_element_type=F32
    )
    grad_state = grad_gated * gate_out

    conv_out, grad_out = conv(signal, grad_state, long_filter)
    conv_state = conv_out + skip_gain[None, :] * signal
    grad_signal = grad_out + skip_gain[None, :] * grad_state

    gated_state = (conv_state * gate_out).astype(BF16)
    partial_value = jnp.dot(gated_state, out_weight, preferred_element_type=F32)
    block_out = lax.psum_scatter(partial_value, "panel", scatter_dimension=1, tiled=True).astype(
        BF16
    )
    grad_gate_out = grad_gated * conv_state
    grad_value = grad_signal * gate_in
    grad_gate_in = grad_signal * value_path
    upstream = jnp.stack([grad_gate_out, grad_gate_in, grad_value])
    after_rim = shifted(upstream[:, : tap_count - 1, :], "seq", -1)
    widened = jnp.concatenate([upstream, after_rim], axis=1)
    grad_projected = short_kernel[0][:, None, :] * widened[:, :row_count, :]
    for tap_index in range(1, tap_count):
        grad_projected = (
            grad_projected
            + short_kernel[tap_index][:, None, :] * widened[:, tap_index : tap_index + row_count, :]
        )
    grad_projected = grad_projected.astype(BF16)
    grad_partial = jnp.einsum("jtc,jdc->td", grad_projected, in_weight, preferred_element_type=F32)
    token_grad = lax.psum_scatter(grad_partial, "panel", scatter_dimension=1, tiled=True).astype(
        BF16
    )
    return (block_out, token_grad)


def solution(mesh):
    placed = (
        P("seq", "panel"),
        P("seq", "panel"),
        P(None, None, "panel"),
        P(None, None, "panel"),
        P("panel"),
        P("seq", "panel"),
        P("panel", None),
    )
    return jax.shard_map(
        local,
        mesh=mesh,
        in_specs=placed,
        out_specs=(P("seq", "panel"), P("seq", "panel")),
        check_vma=False,
    )
```

time: 202 us -> 134 us (0.66)
  starting transfers between devices: 31 us -> 3.84 us
  blocking collectives: 36.4 us -> 17.2 us
  local copies, waits for them, and re-layouts: 9.14 us -> 0.84 us
  Pallas kernels: 51.6 us -> 44.2 us
  waiting for transfers between devices: 48.7 us -> 43.1 us
    all_to_all x2 -> x0, starting transfers between devices: 26.4 us -> none  [the longest x1 15.1 us: local(): lax.all_to_all(long_filter.astype(BF16).T.reshape(n, 4, row_count), 'seq'...]
    all_to_all x1 -> x0, blocking collectives: 20.2 us -> none  [local(): lax.all_to_all(jnp.stack([ys, yg], axis=2), 'seq', 0, 0)]
    all_to_all x2 -> x0, waiting for transfers between devices: 11.2 us -> none  [the longest x1 11.2 us: local(): both = lax.all_to_all(both.reshape(n, 4, 2, row_count), 'seq', 0, 0)]
    pallas_call x1, Pallas kernels: 51.6 us -> 44.2 us  [conv(): pl.pallas_call(functools.partial(conv_kernel, n), out_shape=(out, out), i...]
    reduce_scatter x1, waiting for transfers between devices: 10 us -> 15.6 us  [local(): lax.psum_scatter(partial_value, 'panel', scatter_dimension=1, tiled=True)]
  transfers between devices with their start and end apart: 6 -> 4, of which waited for: 4 -> 3; matrix products, arithmetic and copies ran while one was open for 5% -> 3% of each run, Pallas kernels for 0% -> 0%
where the time goes in v2:
time: 134 us
  Pallas kernels  44.2 us (33%)
  waiting for transfers between devices  43.1 us (32%)
  blocking collectives  17.2 us (13%)
  between operations  14.2 us (11%)
  matrix products  5.74 us (4%)
  other arithmetic  4.74 us (4%)
  starting transfers between devices  3.84 us (3%)
    pallas_call x1, Pallas kernels, conv(): pl.pallas_call(functools.partial(conv_kernel, n), out_shape=(out, out), i...  44.2 us
    reduce_scatter x1, waiting for transfers between devices, local(): lax.psum_scatter(grad_partial, 'panel', scatter_dimension=1, tiled=True)  24.3 us
    reduce_scatter x1, waiting for transfers between devices, local(): lax.psum_scatter(partial_value, 'panel', scatter_dimension=1, tiled=True)  15.6 us
    all_gather x1, blocking collectives, local(): lax.all_gather(tokens, 'panel', axis=1, tiled=True)  9.93 us
    all_gather x1, blocking collectives, local(): lax.all_gather(cotangent, 'panel', axis=1, tiled=True)  7.29 us
    ppermute x2, starting transfers between devices, shifted(): lax.ppermute(value, axis, [(source, source + steps) for source in range(i...  3.76 us
    ppermute x2, waiting for transfers between devices, shifted(): lax.ppermute(value, axis, [(source, source + steps) for source in range(i...  3.08 us
  transfers between devices with their start and end apart: 4, of which 3 were waited for; matrix products, arithmetic and copies ran while one was open for 3% of the time, Pallas kernels for 0%

profile of v2, /device:TPU:1, one launch (start us, length us, event | category | flops | bytes accessed | tf_op | source)
XLA Modules:
  0.0 133.9 jit_solution(13504083079154780280)
XLA Ops:
  7.2 0.0 copy-start
  7.2 0.0 copy-start.6
  7.2 0.0 copy-start.5
  7.2 0.0 reduce-scatter.3.cloned.1.call-start
  7.2 9.9 %all_gather.6 = bf16[256,1024]{1,0:T(8,128)(2,1)S(1)} all-gather(bf16[256,256]{1,0:T(8,128)(2,1)} %param.7), channel_id=1, replica_groups=mesh['seq'=64,'panel'=4] {'panel'}, dimensions={1}, use_global_device_ids=true | all-gather | bytes 655360 | tf_op jit(solution)/shard_map/all_gather | solution.py:234
  17.2 0.0 copy-done
  17.2 0.6 fusion
  17.8 2.5 %collective-permute-start = (bf16[3,2,256]{2,1,0:T(2,128)(2,1)S(1)}, bf16[3,2,256]{2,1,0:T(2,128)(2,1)S(1)}, u32[]{:S(2)}, u32[]{:S(2)}) collective-permute-start(bf16[3,2,256]{2,1,0:T(2,128)(2,1)S(1)} %slice.55), channel_id=1, source_target_pairs={{0,4},{4,8},{8,12},{12,16},{16,20},{20,24},{24,28},{28,32},{32,36}... | collective-permute-start | bytes 9224 | tf_op jit(solution)/shard_map/ppermute | solution.py:227
  20.2 0.0 copy-done.6
  20.3 0.0 copy-done.5
  20.3 7.3 %all_gather.7 = bf16[256,1024]{1,0:T(8,128)(2,1)S(1)} all-gather(bf16[256,256]{1,0:T(8,128)(2,1)S(1)} %copy-done.5), channel_id=1, replica_groups=mesh['seq'=64,'panel'=4] {'panel'}, dimensions={1}, use_global_device_ids=true | all-gather | bytes 655360 | tf_op jit(solution)/shard_map/all_gather | solution.py:235
  27.6 0.0 collective-permute-done
  27.6 0.1 maximum_convert_fusion
  27.7 0.0 copy-start.3
  27.7 0.2 fusion.4
  27.9 0.8 copy-done.3
  28.7 0.0 copy-start.7
  28.7 1.1 fusion.12
  29.8 44.2 %shard_map.86 = (f32[256,256]{1,0:T(8,128)}, f32[256,256]{1,0:T(8,128)}) custom-call(f32[256,256]{1,0:T(8,128)} %get-tuple-element.9.s_ref, f32[256,256]{1,0:T(8,128)} %get-tuple-element.8.g_ref, f32[256,256]{1,0:T(8,128)} %f_ref.1), custom_call_target="tpu_custom_call" | custom-call | tf_op jit(solution)/shard_map/pallas_call | solution.py:197
  74.1 0.0 copy-done.7
  74.1 0.0 copy-start.1
  74.1 0.0 copy-start.2
  74.1 0.0 copy-start.4
  74.1 2.4 %fusion.13 = f32[256,1024]{1,0:T(8,128)} fusion(bf16[256,1024]{1,0:T(8,128)(2,1)S(1)} %copy-done.3, f32[3,256,256]{2,1,0:T(8,128)S(1)} %fusion.4, f32[256,256]{1,0:T(8,128)} %get-tuple-element.4, f32[256,256]{1,0:T(8,128)} %get-tuple-element.9.s_ref, f32[256]{0:T(256)S(1)} %copy-done.7), kind=kOutput, calls=%fused_computation.31 | convolution fusion | flops 134479872 | bytes 2360320 | tf_op jit(solution)/shard_map/dot_general | solution.py:261
  76.5 0.0 reduce-scatter.3.cloned.1.call-update
  76.5 0.0 reduce-scatter.5.cloned.1.call-start
  76.6 0.0 copy-done.1
  76.6 0.0 copy-done.2
  76.6 0.0 copy-done.4
  76.6 1.1 multiply_bitcast_fusion.1
  77.7 0.1 pad_maximum_fusion.1
  77.8 1.3 collective-permute-start.1
  79.1 3.1 %collective-permute-done.1 = f32[3,2,256]{2,1,0:T(2,128)S(1)} collective-permute-done((f32[3,2,256]{2,1,0:T(2,128)S(1)}, f32[3,2,256]{2,1,0:T(2,128)S(1)}, u32[]{:S(2)}, u32[]{:S(2)}) %collective-permute-start.1) | collective-permute-done | bytes 6176 | tf_op jit(solution)/shard_map/ppermute | solution.py:227
  82.1 0.1 pad_maximum_fusion
  82.2 1.7 %convolution_bitcast_fusion = f32[256,1024]{1,0:T(8,128)} fusion(bf16[3,1024,256]{2,1,0:T(8,128)(2,1)S(1)} %copy-done, f32[3,258,256]{2,1,0:T(8,128)S(1)} %pad_maximum_fusion, f32[3,256]{1,0:T(4,128)S(1)} %get-tuple-element.11, f32[3,256]{1,0:T(4,128)S(1)} %get-tuple-element.12, f32[3,256]{1,0:T(4,128)S(1)} %get-tuple-element.10, ...), kind=kOutput, calls=%fused_computation | convolution fusion | flops 404226048 | bytes 4993024 | tf_op jit(solution)/shard_map/jtc,jdc->td/dot_general | solution.py:278
  83.9 0.0 reduce-scatter.5.cloned.1.call-update
  83.9 15.6 %reduce-scatter.3.cloned.1.call-done = f32[256,256]{1,0:T(8,128)} async-done(((f32[256,1024]{1,0:T(8,128)}), f32[256,256]{1,0:T(8,128)}) %reduce-scatter.3.cloned.1.call-update) | async-done | bytes 262160 | tf_op jit(solution)/shard_map/reduce_scatter | solution.py:262
  99.5 1.6 %convert_element_type.25 = bf16[256,256]{1,0:T(8,128)(2,1)} convert(f32[256,256]{1,0:T(8,128)} %reduce-scatter.3.cloned.1.call-done) | non-fusion elementwise | flops 65536 | bytes 393216 | tf_op jit(solution)/shard_map/convert_element_type | solution.py:262
  101.1 24.3 %reduce-scatter.5.cloned.1.call-done = f32[256,256]{1,0:T(8,128)} async-done(((f32[256,1024]{1,0:T(8,128)}), f32[256,256]{1,0:T(8,128)}) %reduce-scatter.5.cloned.1.call-update) | async-done | bytes 262160 | tf_op jit(solution)/shard_map/reduce_scatter | solution.py:279
  125.5 1.6 %convert_element_type.27 = bf16[256,256]{1,0:T(8,128)(2,1)} convert(f32[256,256]{1,0:T(8,128)} %reduce-scatter.5.cloned.1.call-done) | non-fusion elementwise | flops 65536 | bytes 393216 | tf_op jit(solution)/shard_map/convert_element_type | solution.py:279
  (3 shorter events, 0.0 us)
Async XLA Ops:
  7.2 10.0 %copy-start = (bf16[3,1024,256]{2,1,0:T(8,128)(2,1)S(1)}, bf16[3,1024,256]{2,1,0:T(8,128)(2,1)}, u32[]{:S(2)}) copy-start(bf16[3,1024,256]{2,1,0:T(8,128)(2,1)} %param.9) | copy-start | bytes 4718596
  7.2 13.1 %copy-start.6 = (f32[3,3,256]{2,1,0:T(4,128)S(1)}, f32[3,3,256]{2,1,0:T(4,128)}, u32[]{:S(2)}) copy-start(f32[3,3,256]{2,1,0:T(4,128)} %param.10) | copy-start | bytes 27652
  7.2 13.1 %copy-start.5 = (bf16[256,256]{1,0:T(8,128)(2,1)S(1)}, bf16[256,256]{1,0:T(8,128)(2,1)}, u32[]{:S(2)}) copy-start(bf16[256,256]{1,0:T(8,128)(2,1)} %param.8) | copy-start | bytes 393220
  7.2 92.3 %reduce-scatter.3.cloned.1.call-start = ((), (), s32[]{:S(2)}) async-start(), calls=%async_computation.2 | async-start | bytes 1310720 | tf_op jit(solution)/shard_map/reduce_scatter | solution.py:262
  17.8 9.8 %collective-permute-start = (bf16[3,2,256]{2,1,0:T(2,128)(2,1)S(1)}, bf16[3,2,256]{2,1,0:T(2,128)(2,1)S(1)}, u32[]{:S(2)}, u32[]{:S(2)}) collective-permute-start(bf16[3,2,256]{2,1,0:T(2,128)(2,1)S(1)} %slice.55), channel_id=1, source_target_pairs={{0,4},{4,8},{8,12},{12,16},{16,20},{20,24},{24,28},{28,32},{32,36}... | collective-permute-start | bytes 9224 | tf_op jit(solution)/shard_map/ppermute | solution.py:227
  27.7 1.0 copy-start.3
  28.7 45.4 %copy-start.7 = (f32[256]{0:T(256)S(1)}, f32[256]{0:T(256)}, u32[]{:S(2)}) copy-start(f32[256]{0:T(256)} %param.11) | copy-start | bytes 3076
  74.1 2.5 %copy-start.1 = (f32[256,256]{1,0:T(8,128)S(1)}, f32[256,256]{1,0:T(8,128)}, u32[]{:S(2)}) copy-start(f32[256,256]{1,0:T(8,128)} %get-tuple-element.9.s_ref) | copy-start | bytes 786436
  74.1 2.5 %copy-start.2 = (f32[256,256]{1,0:T(8,128)S(1)}, f32[256,256]{1,0:T(8,128)}, u32[]{:S(2)}) copy-start(f32[256,256]{1,0:T(8,128)} %get-tuple-element.8.g_ref) | copy-start | bytes 786436
  74.1 2.5 %copy-start.4 = (f32[256,256]{1,0:T(8,128)S(1)}, f32[256,256]{1,0:T(8,128)}, u32[]{:S(2)}) copy-start(f32[256,256]{1,0:T(8,128)} %get-tuple-element.4) | copy-start | bytes 786436
  76.5 48.9 %reduce-scatter.5.cloned.1.call-start = ((), (), s32[]{:S(2)}) async-start(), calls=%async_computation.3 | async-start | bytes 1310720 | tf_op jit(solution)/shard_map/reduce_scatter | solution.py:279
  77.8 4.4 %collective-permute-start.1 = (f32[3,2,256]{2,1,0:T(2,128)S(1)}, f32[3,2,256]{2,1,0:T(2,128)S(1)}, u32[]{:S(2)}, u32[]{:S(2)}) collective-permute-start(f32[3,2,256]{2,1,0:T(2,128)S(1)} %slice.62), channel_id=1, source_target_pairs={{4,0},{8,4},{12,8},{16,12},{20,16},{24,20},{28,24},{32,28},{36,32}... | collective-permute-start | bytes 18440 | tf_op jit(solution)/shard_map/ppermute | solution.py:227
Sparse Core Ops, SparseCore 0:
  76.7 22.7 reduce-scatter.2
  102.2 23.2 reduce-scatter.4

commit v3 on v2

--- a/solution.py
+++ b/solution.py
@@ -137,29 +137,119 @@
     ys[...] = yf[...].reshape(64, 16, 128).astype(BF16)
 
 
-def conv_kernel(
-    n, s_ref, g_ref, f_ref, so_ref, go_ref, hs, hr, xs, xr, xf, xl, tot, r_ref, yf, ys, yr, hsem, xsem, ysem
+def block_kernel(
+    n, tok, cot, w_in_hbm, taps, skip, filt, w_out_hbm, out_ref, grad_ref,
+    w_in, w_out, tokb, cotb, ext, gate, sig, gg, gs, hs, hr, xs, xr, xf, xl, tot, r_ref, yf, ys, yr,
+    ups, edge, gp, own, half_send, half_recv, sum_send, sum_recv,
+    wsem, tsem, fsem, esem, csem, hsem, xsem, ysem, usem, rsem, qsem,
 ):
-    me = lax.axis_index("seq")
+    me, p = lax.axis_index("seq"), lax.axis_index("panel")
+    core, chip = lax.rem(p, 2), p // 2
+    sibling = chip * 2 + 1 - core
+    across = (1 - chip) * 2 + core
+    diagonal = (1 - chip) * 2 + 1 - core
+    later, earlier = lax.rem(me + 1, n), lax.rem(me + n - 1, n)
+
+    load_in = pltpu.make_async_copy(w_in_hbm, w_in, wsem.at[0])
+    load_out = pltpu.make_async_copy(w_out_hbm, w_out, wsem.at[1])
+    load_in.start()
+    load_out.start()
+
     barrier = pltpu.get_barrier_semaphore()
 
+    def signal(seq, panel):
+        pl.semaphore_signal(
+            barrier, inc=1, device_id={"seq": seq, "panel": panel}, device_id_type=MESH
+        )
+
+    signal(me, sibling)
+    signal(me, across)
+    for other in (sibling, across, diagonal):
+        signal(earlier, other)
+
     def greet(j, carry):
-        pl.semaphore_signal(
-            barrier, inc=1, device_id={"seq": lax.rem(me + j, n)}, device_id_type=MESH
+        signal(lax.rem(me + j, n), p)
+        return carry
+
+    lax.fori_loop(1, n, greet, 0)
+
+    def send(src, dst, sems, seq, panel):
+        copy = pltpu.make_async_remote_copy(
+            src_ref=src,
+            dst_ref=dst,
+            send_sem=sems.at[0],
+            recv_sem=sems.at[1],
+            device_id={"seq": seq, "panel": panel},
+            device_id_type=MESH,
         )
-        return carry
-
-    lax.fori_loop(1, n, greet, 0)
+        copy.start()
+        return copy
+
     eye, flip = identity(False), identity(True)
-    ft = turn(eye, f_ref[...].astype(BF16))
+    ft = turn(eye, filt[...].astype(BF16))
     even, odd = interleave(ft[:, :128], ft[:, 128:])
     hs[...] = jnp.stack([even, odd], axis=1).reshape(64, 8, 128)
     hr[0] = jnp.zeros((8, 128), F32)
-    pl.semaphore_wait(barrier, n - 1)
+    tokb[p, 16:272, :] = tok[...]
+    cotb[p] = cot[...]
+    pl.semaphore_wait(barrier, n + 4)
+
+    body = pl.ds(16, 256)
+    rim = pl.ds(0, 16)
+    tok_across = send(tok, tokb.at[p, body], tsem.at[0], me, across)
+    tok_sibling = send(tok, tokb.at[p, body], tsem.at[1], me, sibling)
+    edges = [
+        send(tok.at[pl.ds(240, 16)], tokb.at[p, rim], esem.at[slot], later, panel)
+        for slot, panel in enumerate((p, sibling, across, diagonal))
+    ]
+    cot_across = send(cot, cotb.at[p], csem.at[0], me, across)
+    cot_sibling = send(cot, cotb.at[p], csem.at[1], me, sibling)
     exchange(n, hs, hr, 1, hsem)
-
-    st = turn(eye, s_ref[...].astype(BF16))
-    gf = jnp.dot(flip, g_ref[...].astype(BF16), preferred_element_type=F32)
+    tok_across.wait_recv()
+    tok_forward = send(tokb.at[across, body], tokb.at[across, body], fsem.at[0], me, sibling)
+    tok_sibling.wait_recv()
+    for copy in edges:
+        copy.wait_recv()
+    tok_forward.wait_recv()
+    load_in.wait()
+
+    started = (me > 0).astype(F32)
+    for j in range(3):
+        value = None
+        for k in range(4):
+            part = jnp.dot(
+                tokb[k], w_in[j, 256 * k : 256 * (k + 1), :], preferred_element_type=F32
+            )
+            value = part if value is None else value + part
+        value = value.astype(BF16).astype(F32)
+        ext[j, 0:16, :] = value[0:16] * started
+        ext[j, 16:272, :] = value[16:]
+    for j in range(3):
+        gate[j] = (
+            taps[0, j : j + 1, :] * ext[j, 16:272, :]
+            + taps[1, j : j + 1, :] * ext[j, 15:271, :]
+            + taps[2, j : j + 1, :] * ext[j, 14:270, :]
+        )
+    sig[...] = gate[2] * gate[1]
+    st = turn(eye, sig[...].astype(BF16))
+
+    cot_across.wait_recv()
+    cot_forward = send(cotb.at[across], cotb.at[across], fsem.at[1], me, sibling)
+    cot_sibling.wait_recv()
+    cot_forward.wait_recv()
+    load_out.wait()
+    value = None
+    for k in range(4):
+        part = lax.dot_general(
+            cotb[k],
+            w_out[:, 256 * k : 256 * (k + 1)],
+            (((1,), (1,)), ((), ())),
+            preferred_element_type=F32,
+        )
+        value = part if value is None else value + part
+    gg[...] = value
+    gs[...] = value * gate[0]
+    gf = jnp.dot(flip, gs[...].astype(BF16), preferred_element_type=F32)
     gt = turn(eye, gf.astype(BF16))
     even_lo, odd_lo = interleave(st[:, :128], gt[:, :128])
     even_hi, odd_hi = interleave(st[:, 128:], gt[:, 128:])
@@ -183,23 +273,88 @@
         odd = back[:, 1, 8 * half : 8 * half + 8]
         cols_s.append(jnp.where(upper, even, pltpu.roll(odd, 4, 1)).reshape(256, 128))
         cols_g.append(jnp.where(upper, pltpu.roll(even, 4, 1), odd).reshape(256, 128))
-    so_ref[...] = turn(eye, jnp.concatenate(cols_s, axis=1).astype(BF16))
-    go_ref[...] = turn(flip, jnp.concatenate(cols_g, axis=1).astype(BF16))
+    state = turn(eye, jnp.concatenate(cols_s, axis=1).astype(BF16)) + skip[...] * sig[...]
+    grad_signal = turn(flip, jnp.concatenate(cols_g, axis=1).astype(BF16)) + skip[...] * gs[...]
+    ups[0, 0:256, :] = gg[...] * state
+    ups[1, 0:256, :] = grad_signal * gate[2]
+    ups[2, 0:256, :] = grad_signal * gate[1]
+    rim_copy = send(ups.at[:, pl.ds(0, 8)], edge, usem, earlier, p)
+
+    def scatter_sum(which, product):
+        half_send[which, 0] = product(sibling).astype(BF16)
+        half_send[which, 1] = product(diagonal).astype(BF16)
+        first = send(half_send.at[which], half_recv.at[which], rsem.at[which], me, sibling)
+        own[which] = product(p)
+        value = product(across)
+        first.wait_recv()
+        sum_send[which] = (value + half_recv[which, 1].astype(F32)).astype(BF16)
+        second = send(sum_send.at[which], sum_recv.at[which], qsem.at[which], me, across)
+        own[which] = own[which] + half_recv[which, 0].astype(F32)
+        return first, second
+
+    gated = (state * gate[0]).astype(BF16)
+
+    def out_product(k):
+        cols = pl.ds(pl.multiple_of(k * 256, 256), 256)
+        return jnp.dot(gated, w_out[:, cols], preferred_element_type=F32)
+
+    sent = scatter_sum(0, out_product)
+
+    rim_copy.wait_recv()
+    ups[:, 256:264, :] = edge[...] * (me < n - 1).astype(F32)
+    for j in range(3):
+        gp[j] = (
+            taps[0, j : j + 1, :] * ups[j, 0:256, :]
+            + taps[1, j : j + 1, :] * ups[j, 1:257, :]
+            + taps[2, j : j + 1, :] * ups[j, 2:258, :]
+        ).astype(BF16)
+
+    def grad_product(k):
+        rows = pl.ds(pl.multiple_of(k * 256, 256), 256)
+        value = None
+        for j in range(3):
+            part = lax.dot_general(
+                gp[j], w_in[j, rows, :], (((1,), (1,)), ((), ())), preferred_element_type=F32
+            )
+            value = part if value is None else value + part
+        return value
+
+    sent = sent + scatter_sum(1, grad_product)
+    sent[1].wait_recv()
+    out_ref[...] = (own[0] + sum_recv[0].astype(F32)).astype(BF16)
+    sent[3].wait_recv()
+    grad_ref[...] = (own[1] + sum_recv[1].astype(F32)).astype(BF16)
+
+    for copy in (tok_across, tok_sibling, tok_forward, cot_across, cot_sibling, cot_forward, rim_copy):
+        copy.wait_send()
+    for copy in tuple(edges) + sent:
+        copy.wait_send()
     await_all(n, hr, hsem.at[0])
     await_all(n, xr, xsem.at[0])
     await_all(n, yr, ysem.at[0])
 
 
-def conv(signal, grad_state, long_filter):
+def local(tokens, cotangent, in_weight, short_kernel, skip_gain, long_filter, out_weight):
     n = lax.axis_size("seq")
-    out = jax.ShapeDtypeStruct((256, 256), F32)
+    out = jax.ShapeDtypeStruct((256, 256), BF16)
     vmem = pl.BlockSpec(memory_space=pltpu.VMEM)
+    hbm = pl.BlockSpec(memory_space=pl.ANY)
+    sem = pltpu.SemaphoreType.DMA
     return pl.pallas_call(
-        functools.partial(conv_kernel, n),
+        functools.partial(block_kernel, n),
         out_shape=(out, out),
-        in_specs=[vmem] * 3,
+        in_specs=[vmem, vmem, hbm, vmem, vmem, vmem, hbm],
         out_specs=(vmem, vmem),
         scratch_shapes=[
+            pltpu.VMEM((3, 1024, 256), BF16),
+            pltpu.VMEM((256, 1024), BF16),
+            pltpu.VMEM((4, 272, 256), BF16),
+            pltpu.VMEM((4, 256, 256), BF16),
+            pltpu.VMEM((3, 272, 256), F32),
+            pltpu.VMEM((3, 256, 256), F32),
+            pltpu.VMEM((256, 256), F32),
+            pltpu.VMEM((256, 256), F32),
+            pltpu.VMEM((256, 256), F32),
             pltpu.VMEM((64, 8, 128), F32),
             pltpu.VMEM((65, 8, 128), F32),
             pltpu.VMEM((64, 16, 128), BF16),
@@ -211,75 +366,38 @@
             pltpu.VMEM((1024, 128), F32),
             pltpu.VMEM((64, 16, 128), BF16),
             pltpu.VMEM((64, 16, 128), BF16),
-            pltpu.SemaphoreType.DMA((2,)),
-            pltpu.SemaphoreType.DMA((2,)),
-            pltpu.SemaphoreType.DMA((2,)),
+            pltpu.VMEM((3, 264, 256), F32),
+            pltpu.VMEM((3, 8, 256), F32),
+            pltpu.VMEM((3, 256, 256), BF16),
+            pltpu.VMEM((2, 256, 256), F32),
+            pltpu.VMEM((2, 2, 256, 256), BF16),
+            pltpu.VMEM((2, 2, 256, 256), BF16),
+            pltpu.VMEM((2, 256, 256), BF16),
+            pltpu.VMEM((2, 256, 256), BF16),
+            sem((2,)),
+            sem((2, 2)),
+            sem((2, 2)),
+            sem((4, 2)),
+            sem((2, 2)),
+            sem((2,)),
+            sem((2,)),
+            sem((2,)),
+            sem((2,)),
+            sem((2, 2)),
+            sem((2, 2)),
         ],
         compiler_params=pltpu.CompilerParams(
-            collective_id=0, has_side_effects=True, vmem_limit_bytes=56 * 2**20
+            collective_id=0, has_side_effects=True, vmem_limit_bytes=58 * 2**20
         ),
-    )(signal, grad_state, long_filter)
-
-
-def shifted(value, axis, steps):
-    count = lax.axis_size(axis)
-    initial, last = (max(0, -steps), min(count, count - steps))
-    return lax.ppermute(value, axis, [(source, source + steps) for source in range(initial, last)])
-
-
-def local(tokens, cotangent, in_weight, short_kernel, skip_gain, long_filter, out_weight):
-    row_count = tokens.shape[0]
-    tap_count = short_kernel.shape[0]
-    full_tok, full_cot = (
-        lax.all_gather(tokens, "panel", axis=1, tiled=True),
-        lax.all_gather(cotangent, "panel", axis=1, tiled=True),
+    )(
+        tokens,
+        cotangent,
+        in_weight,
+        short_kernel,
+        skip_gain.reshape(1, -1),
+        long_filter,
+        out_weight,
     )
-    projected = jnp.einsum(
-        "td,jdc->jtc", full_tok, in_weight, preferred_element_type=F32
-    ).astype(BF16)
-    before = shifted(projected[:, row_count - (tap_count - 1) :, :], "seq", 1)
-    extended = jnp.concatenate([before, projected], axis=1).astype(F32)
-    filtered = short_kernel[0][:, None, :] * extended[:, tap_count - 1 :, :]
-    for tap_index in range(1, tap_count):
-        filtered = (
-            filtered
-            + short_kernel[tap_index][:, None, :]
-            * extended[:, tap_count - 1 - tap_index : tap_count - 1 - tap_index + row_count, :]
-        )
-    gate_out, gate_in, value_path = (filtered[0], filtered[1], filtered[2])
-    signal = value_path * gate_in
-    grad_gated = lax.dot_general(
-        full_cot, out_weight, (((1,), (1,)), ((), ())), preferred_element_type=F32
-    )
-    grad_state = grad_gated * gate_out
-
-    conv_out, grad_out = conv(signal, grad_state, long_filter)
-    conv_state = conv_out + skip_gain[None, :] * signal
-    grad_signal = grad_out + skip_gain[None, :] * grad_state
-
-    gated_state = (conv_state * gate_out).astype(BF16)
-    partial_value = jnp.dot(gated_state, out_weight, preferred_element_type=F32)
-    block_out = lax.psum_scatter(partial_value, "panel", scatter_dimension=1, tiled=True).astype(
-        BF16
-    )
-    grad_gate_out = grad_gated * conv_state
-    grad_value = grad_signal * gate_in
-    grad_gate_in = grad_signal * value_path
-    upstream = jnp.stack([grad_gate_out, grad_gate_in, grad_value])
-    after_rim = shifted(upstream[:, : tap_count - 1, :], "seq", -1)
-    widened = jnp.concatenate([upstream, after_rim], axis=1)
-    grad_projected = short_kernel[0][:, None, :] * widened[:, :row_count, :]
-    for tap_index in range(1, tap_count):
-        grad_projected = (
-            grad_projected
-            + short_kernel[tap_index][:, None, :] * widened[:, tap_index : tap_index + row_count, :]
-        )
-    grad_projected = grad_projected.astype(BF16)
-    grad_partial = jnp.einsum("jtc,jdc->td", grad_projected, in_weight, preferred_element_type=F32)
-    token_grad = lax.psum_scatter(grad_partial, "panel", scatter_dimension=1, tiled=True).astype(
-        BF16
-    )
-    return (block_out, token_grad)
 
 
 def solution(mesh):

time: 134 us -> 67.1 us (0.50)
  waiting for transfers between devices: 43.1 us -> 0 us
  Pallas kernels: 44.2 us -> 63.2 us
  blocking collectives: 17.2 us -> 0 us
  between operations: 14.2 us -> 0.64 us
  matrix products: 5.74 us -> 0 us
  other arithmetic: 4.74 us -> 0 us
  starting transfers between devices: 3.84 us -> 0 us
  local copies, waits for them, and re-layouts: 0.84 us -> 3.14 us
    reduce_scatter x2 -> x0, waiting for transfers between devices: 40 us -> none  [the longest x1 24.3 us: local(): lax.psum_scatter(grad_partial, 'panel', scatter_dimension=1, tiled=True)]
    pallas_call x1, Pallas kernels: 44.2 us -> 63.2 us  [local(): pl.pallas_call(functools.partial(block_kernel, n), out_shape=(out, out),...]
    all_gather x2 -> x0, blocking collectives: 17.2 us -> none  [the longest x1 9.93 us: local(): lax.all_gather(tokens, 'panel', axis=1, tiled=True)]
    dot_general x4 -> x0, matrix products: 5.74 us -> none  [the longest x1 2.39 us: local(): partial_value = jnp.dot(gated_state, out_weight, preferred_element_type=F32)]
    ppermute x2 -> x0, starting transfers between devices: 3.76 us -> none  [shifted(): lax.ppermute(value, axis, [(source, source + steps) for source in range(i...]
    convert_element_type x3 -> x0, other arithmetic: 3.32 us -> none  [the longest x1 1.62 us: local(): lax.psum_scatter(partial_value, 'panel', scatter_dimension=1, tiled=True)]
    ppermute x2 -> x0, waiting for transfers between devices: 3.08 us -> none  [shifted(): lax.ppermute(value, axis, [(source, source + steps) for source in range(i...]
    unnamed x16 -> x2, local copies, waits for them, and re-layouts: 0.83 us -> 3.14 us
  transfers between devices with their start and end apart: 4 -> 0, of which waited for: 3 -> 0; matrix products, arithmetic and copies ran while one was open for 3% -> 0% of each run, Pallas kernels for 0% -> 0%
where the time goes in v3:
time: 67.1 us; the launch traced here: 66.9 us
  Pallas kernels  63.2 us (94%)
  local copies, waits for them, and re-layouts  3.14 us (5%)
    pallas_call x1, Pallas kernels, local(): pl.pallas_call(functools.partial(block_kernel, n), out_shape=(out, out),...  63.2 us
    unnamed x2, local copies, waits for them, and re-layouts  3.14 us

profile of v3, /device:TPU:1, one launch (start us, length us, event | category | flops | bytes accessed | tf_op | source)
XLA Modules:
  0.0 66.9 jit_solution(16820953797429712858)
XLA Ops:
  0.6 63.2 %shard_map.86 = (bf16[256,256]{1,0:T(8,128)(2,1)}, bf16[256,256]{1,0:T(8,128)(2,1)}) custom-call(bf16[256,256]{1,0:T(8,128)(2,1)} %tok.1, bf16[256,256]{1,0:T(8,128)(2,1)} %cot.1, bf16[3,1024,256]{2,1,0:T(8,128)(2,1)} %w_in_hbm.1, f32[3,3,256]{2,1,0:T(4,128)} %taps.1, f32[1,256]{1,0:T(1,128)} %bitcast.1, f32[256,256]{1,0:T(8,128)} %filt.1, ...), custom_call_target="tpu_custom_call" | custom-call | tf_op jit(solution)/shard_map/pallas_call | solution.py:343
  63.8 1.6 %copy.11 = bf16[256,256]{1,0:T(8,128)(2,1)} copy(bf16[256,256]{1,0:T(8,128)(2,1)} %get-tuple-element.4) | data formatting | bytes 262144
  65.4 1.6 %copy.12 = bf16[256,256]{1,0:T(8,128)(2,1)} copy(bf16[256,256]{1,0:T(8,128)(2,1)} %get-tuple-element.5) | data formatting | bytes 262144

commit v4 on v3

--- a/solution.py
+++ b/solution.py
@@ -23,12 +23,24 @@
     return lax.dot_general(select, value, (((1,), (1,)), ((), ())), preferred_element_type=F32)
 
 
-def interleave(first, second):
-    first, second = first.reshape(32, 8, 128), second.reshape(32, 8, 128)
-    upper = lax.broadcasted_iota(jnp.int32, (32, 8, 128), 1) < 4
-    even = jnp.where(upper, first, pltpu.roll(second, 4, 1))
-    odd = jnp.where(upper, pltpu.roll(first, 4, 1), second)
-    return even, odd
+def spread():
+    half = lax.broadcasted_iota(jnp.int32, (2, 512, 256), 0)
+    row = lax.broadcasted_iota(jnp.int32, (2, 512, 256), 1)
+    col = lax.broadcasted_iota(jnp.int32, (2, 512, 256), 2)
+    return jnp.where(col + (col // 4) * 4 + 4 * half == row, 1.0, 0.0).astype(BF16)
+
+
+def collect(pair):
+    row = lax.broadcasted_iota(jnp.int32, (1024, 512), 0)
+    col = lax.broadcasted_iota(jnp.int32, (1024, 512), 1)
+    channel = row % 256
+    source = (channel // 4) * 8 + 2 * (row // 256) + channel % 2
+    return jnp.where((col == source) & ((channel // 2) % 2 == pair), 1.0, 0.0).astype(BF16)
+
+
+def chunks(spread_ref, value):
+    rows = turn(spread_ref[0], value[:128]) + turn(spread_ref[1], value[128:])
+    return rows.reshape(64, 8, 128).astype(BF16)
 
 
 def exchange(n, send_ref, recv_ref, offset, sems):
@@ -46,7 +58,7 @@
         ).start()
         return carry
 
-    lax.fori_loop(1, n, one, 0)
+    lax.fori_loop(1, n, one, 0, unroll=9)
     recv_ref[me + offset] = send_ref[me]
 
 
@@ -55,42 +67,37 @@
     pltpu.make_async_copy(part, part, sem).wait()
 
 
-def build_toeplitz(hr, r_ref):
+def build_toeplitz(hc, r_ref, first, last):
     row = lax.broadcasted_iota(jnp.int32, (128, 128), 0)
     col = lax.broadcasted_iota(jnp.int32, (128, 128), 1)
     cut = col >= 128 - row
 
     def channel(c, carry):
         r_ref[c, 128:256, 0:128] = jnp.zeros((128, 128), BF16)
-
-        def block(a, carry):
-            early = jnp.broadcast_to(hr[a, pl.ds(c + 4, 1), :], (128, 128))
-            for half in range(2):
-                now = jnp.broadcast_to(hr[a + 1, pl.ds(c + 4 * half, 1), :], (128, 128))
-                mixed = jnp.where(cut, early, now)
-                tile = pltpu.roll(mixed, 0, 1, stride=1, stride_axis=0).astype(BF16)
-                at = pl.multiple_of(a * 256, 256) + 128 * half
-                r_ref[c, 0:128, pl.ds(at, 128)] = tile
-                r_ref[c, 128:256, pl.ds(at + 128, 128)] = tile
-                early = now
-            return carry
-
-        lax.fori_loop(0, 64, block, 0, unroll=8)
+        early = jnp.zeros((128, 128), F32)
+        for k in range(128):
+            now = jnp.broadcast_to(hc[c, k : k + 1, :], (128, 128))
+            mixed = jnp.where(cut, early, now)
+            tile = pltpu.roll(mixed, 0, 1, stride=1, stride_axis=0).astype(BF16)
+            at = 128 * k
+            r_ref[c, 0:128, at : at + 128] = tile
+            r_ref[c, 128:256, at + 128 : at + 256] = tile
+            early = now
         return carry
 
-    lax.fori_loop(0, 4, channel, 0)
-
-
-def convolve(xr, xf, xl, tot, r_ref, yf, ys):
-    xf[...] = xr[...].astype(F32).reshape(1024, 128)
+    lax.fori_loop(first, last, channel, 0)
+
+
+def shifted_blocks(sr, gr, sf, gf, xl):
+    sf[...] = sr[...].astype(F32).reshape(512, 128)
+    gf[...] = gr[...].astype(F32).reshape(512, 128)
     for c in range(4):
         rows = []
         for j in range(8):
-            s_at, g_at = 128 * j + c, 128 * (7 - j) + 4 + c
-            for at in (s_at, g_at):
+            for ref, at in ((sf, 64 * j + c), (gf, 64 * (7 - j) + c)):
                 rows.append(
                     jnp.concatenate(
-                        [xf[pl.ds(at, 8, stride=16), :], xf[pl.ds(at + 8, 8, stride=16), :]], axis=1
+                        [ref[pl.ds(at, 8, stride=8), :], ref[pl.ds(at + 4, 8, stride=8), :]], axis=1
                     )
                 )
         x = jnp.concatenate(rows, axis=0).astype(BF16)
@@ -99,9 +106,12 @@
             xl[c, 0 : 16 * q, 256 * q : 256 * (q + 1)] = jnp.zeros((16 * q, 256), BF16)
             xl[c, 16 * q :, 256 * q : 256 * (q + 1)] = x[: 128 - 16 * q]
 
+
+def convolve(pair, xl, r_ref, yf, ys):
     sub = lax.broadcasted_iota(jnp.int32, (8, 8, 256), 1)
 
-    def channel(c, carry):
+    def channel(t, carry):
+        c = 2 * pair + t
         total = [None, None]
         for r in range(8):
             z = None
@@ -124,24 +134,21 @@
                 inside = sub >= r if side == 0 else sub < 8 - r
                 total[side] = total[side] + jnp.where(inside, turned, before)
         for side in range(2):
-            tot[c, side] = total[side]
+            for j in range(8):
+                at = 64 * (j if side == 0 else 7 - j) + 2 * side
+                yf[pl.ds(at + t, 8, stride=8), :] = total[side][j, :, 0:128]
+                yf[pl.ds(at + 4 + t, 8, stride=8), :] = total[side][j, :, 128:256]
         return carry
 
-    lax.fori_loop(0, 4, channel, 0)
-    for c in range(4):
-        for j in range(8):
-            s_at, g_at = 128 * j + c, 128 * (7 - j) + 4 + c
-            for side, at in ((0, s_at), (1, g_at)):
-                yf[pl.ds(at, 8, stride=16), :] = tot[c, side, j, :, 0:128]
-                yf[pl.ds(at + 8, 8, stride=16), :] = tot[c, side, j, :, 128:256]
-    ys[...] = yf[...].reshape(64, 16, 128).astype(BF16)
+    lax.fori_loop(0, 2, channel, 0)
+    ys[pair] = yf[...].reshape(64, 8, 128).astype(BF16)
 
 
 def block_kernel(
     n, tok, cot, w_in_hbm, taps, skip, filt, w_out_hbm, out_ref, grad_ref,
-    w_in, w_out, tokb, cotb, ext, gate, sig, gg, gs, hs, hr, xs, xr, xf, xl, tot, r_ref, yf, ys, yr,
+    w_in, w_out, tokb, cotb, ext, gate, sig, gg, gs, es, cs, hs, hr, hf, hc, ss, sr, sf, gx, gr, gf, xl, r_ref, yf, ys, yr,
     ups, edge, gp, own, half_send, half_recv, sum_send, sum_recv,
-    wsem, tsem, fsem, esem, csem, hsem, xsem, ysem, usem, rsem, qsem,
+    wsem, tsem, fsem, esem, csem, hsem, ssem, gsem, ysem, usem, rsem, qsem,
 ):
     me, p = lax.axis_index("seq"), lax.axis_index("panel")
     core, chip = lax.rem(p, 2), p // 2
@@ -171,7 +178,7 @@
         signal(lax.rem(me + j, n), p)
         return carry
 
-    lax.fori_loop(1, n, greet, 0)
+    lax.fori_loop(1, n, greet, 0, unroll=9)
 
     def send(src, dst, sems, seq, panel):
         copy = pltpu.make_async_remote_copy(
@@ -185,13 +192,6 @@
         copy.start()
         return copy
 
-    eye, flip = identity(False), identity(True)
-    ft = turn(eye, filt[...].astype(BF16))
-    even, odd = interleave(ft[:, :128], ft[:, 128:])
-    hs[...] = jnp.stack([even, odd], axis=1).reshape(64, 8, 128)
-    hr[0] = jnp.zeros((8, 128), F32)
-    tokb[p, 16:272, :] = tok[...]
-    cotb[p] = cot[...]
     pl.semaphore_wait(barrier, n + 4)
 
     body = pl.ds(16, 256)
@@ -202,9 +202,17 @@
         send(tok.at[pl.ds(240, 16)], tokb.at[p, rim], esem.at[slot], later, panel)
         for slot, panel in enumerate((p, sibling, across, diagonal))
     ]
+    es[...] = spread()
+    hs[...] = chunks(es, filt[...].astype(BF16))
+    hr[0] = jnp.zeros((8, 128), BF16)
+    exchange(n, hs, hr, 1, hsem)
     cot_across = send(cot, cotb.at[p], csem.at[0], me, across)
     cot_sibling = send(cot, cotb.at[p], csem.at[1], me, sibling)
-    exchange(n, hs, hr, 1, hsem)
+    tokb[p, 16:272, :] = tok[...]
+    cotb[p] = cot[...]
+    cs[0] = collect(0)
+    cs[1] = collect(1)
+    eye, flip = identity(False), identity(True)
     tok_across.wait_recv()
     tok_forward = send(tokb.at[across, body], tokb.at[across, body], fsem.at[0], me, sibling)
     tok_sibling.wait_recv()
@@ -231,7 +239,13 @@
             + taps[2, j : j + 1, :] * ext[j, 14:270, :]
         )
     sig[...] = gate[2] * gate[1]
-    st = turn(eye, sig[...].astype(BF16))
+    ss[...] = chunks(es, sig[...].astype(BF16))
+    exchange(n, ss, sr, 0, ssem)
+    await_all(n, hr, hsem.at[1])
+    hf[...] = hr[...].astype(F32).reshape(520, 128)
+    for c in range(4):
+        hc[c] = hf[pl.ds(8 + c, 128, stride=4), :]
+    build_toeplitz(hc, r_ref, 0, 1)
 
     cot_across.wait_recv()
     cot_forward = send(cotb.at[across], cotb.at[across], fsem.at[1], me, sibling)
@@ -249,32 +263,27 @@
         value = part if value is None else value + part
     gg[...] = value
     gs[...] = value * gate[0]
-    gf = jnp.dot(flip, gs[...].astype(BF16), preferred_element_type=F32)
-    gt = turn(eye, gf.astype(BF16))
-    even_lo, odd_lo = interleave(st[:, :128], gt[:, :128])
-    even_hi, odd_hi = interleave(st[:, 128:], gt[:, 128:])
-    even = jnp.concatenate([even_lo, even_hi], axis=1)
-    odd = jnp.concatenate([odd_lo, odd_hi], axis=1)
-    xs[...] = jnp.stack([even, odd], axis=1).reshape(64, 16, 128).astype(BF16)
-    exchange(n, xs, xr, 0, xsem)
-
-    await_all(n, hr, hsem.at[1])
-    build_toeplitz(hr, r_ref)
-    await_all(n, xr, xsem.at[1])
-    convolve(xr, xf, xl, tot, r_ref, yf, ys)
-    exchange(n, ys, yr, 0, ysem)
-    await_all(n, yr, ysem.at[1])
-
-    back = yr[...].astype(F32).reshape(32, 2, 16, 128)
-    upper = lax.broadcasted_iota(jnp.int32, (32, 8, 128), 1) < 4
-    cols_s, cols_g = [], []
-    for half in range(2):
-        even = back[:, 0, 8 * half : 8 * half + 8]
-        odd = back[:, 1, 8 * half : 8 * half + 8]
-        cols_s.append(jnp.where(upper, even, pltpu.roll(odd, 4, 1)).reshape(256, 128))
-        cols_g.append(jnp.where(upper, pltpu.roll(even, 4, 1), odd).reshape(256, 128))
-    state = turn(eye, jnp.concatenate(cols_s, axis=1).astype(BF16)) + skip[...] * sig[...]
-    grad_signal = turn(flip, jnp.concatenate(cols_g, axis=1).astype(BF16)) + skip[...] * gs[...]
+    turned = jnp.dot(flip, gs[...].astype(BF16), preferred_element_type=F32).astype(BF16)
+    gx[...] = chunks(es, turned)
+    exchange(n, gx, gr, 0, gsem)
+
+    build_toeplitz(hc, r_ref, 1, 4)
+    await_all(n, sr, ssem.at[1])
+    await_all(n, gr, gsem.at[1])
+    shifted_blocks(sr, gr, sf, gf, xl)
+    for pair in range(2):
+        convolve(pair, xl, r_ref, yf, ys)
+        exchange(n, ys.at[pair], yr.at[pair], 0, ysem.at[pair])
+    back = None
+    for pair in range(2):
+        await_all(n, yr.at[pair], ysem.at[pair, 1])
+        part = jnp.dot(cs[pair], yr[pair].reshape(512, 128), preferred_element_type=F32)
+        back = part if back is None else back + part
+    back = back.astype(BF16)
+    state = jnp.concatenate([back[0:256], back[512:768]], axis=1)
+    grad_signal = jnp.concatenate([back[256:512], back[768:1024]], axis=1)
+    state = turn(eye, state) + skip[...] * sig[...]
+    grad_signal = turn(flip, grad_signal) + skip[...] * gs[...]
     ups[0, 0:256, :] = gg[...] * state
     ups[1, 0:256, :] = grad_signal * gate[2]
     ups[2, 0:256, :] = grad_signal * gate[1]
@@ -330,8 +339,10 @@
     for copy in tuple(edges) + sent:
         copy.wait_send()
     await_all(n, hr, hsem.at[0])
-    await_all(n, xr, xsem.at[0])
-    await_all(n, yr, ysem.at[0])
+    await_all(n, sr, ssem.at[0])
+    await_all(n, gr, gsem.at[0])
+    await_all(n, yr.at[0], ysem.at[0, 0])
+    await_all(n, yr.at[1], ysem.at[1, 0])
 
 
 def local(tokens, cotangent, in_weight, short_kernel, skip_gain, long_filter, out_weight):
@@ -355,17 +366,23 @@
             pltpu.VMEM((256, 256), F32),
             pltpu.VMEM((256, 256), F32),
             pltpu.VMEM((256, 256), F32),
-            pltpu.VMEM((64, 8, 128), F32),
-            pltpu.VMEM((65, 8, 128), F32),
-            pltpu.VMEM((64, 16, 128), BF16),
-            pltpu.VMEM((64, 16, 128), BF16),
-            pltpu.VMEM((1024, 128), F32),
+            pltpu.VMEM((2, 512, 256), BF16),
+            pltpu.VMEM((2, 1024, 512), BF16),
+            pltpu.VMEM((64, 8, 128), BF16),
+            pltpu.VMEM((65, 8, 128), BF16),
+            pltpu.VMEM((520, 128), F32),
+            pltpu.VMEM((4, 128, 128), F32),
+            pltpu.VMEM((64, 8, 128), BF16),
+            pltpu.VMEM((64, 8, 128), BF16),
+            pltpu.VMEM((512, 128), F32),
+            pltpu.VMEM((64, 8, 128), BF16),
+            pltpu.VMEM((64, 8, 128), BF16),
+            pltpu.VMEM((512, 128), F32),
             pltpu.VMEM((4, 128, 2048), BF16),
-            pltpu.VMEM((4, 2, 8, 8, 256), F32),
             pltpu.VMEM((4, 256, 16384 + 128), BF16),
-            pltpu.VMEM((1024, 128), F32),
-            pltpu.VMEM((64, 16, 128), BF16),
-            pltpu.VMEM((64, 16, 128), BF16),
+            pltpu.VMEM((512, 128), F32),
+            pltpu.VMEM((2, 64, 8, 128), BF16),
+            pltpu.VMEM((2, 64, 8, 128), BF16),
             pltpu.VMEM((3, 264, 256), F32),
             pltpu.VMEM((3, 8, 256), F32),
             pltpu.VMEM((3, 256, 256), BF16),
@@ -382,6 +399,7 @@
             sem((2,)),
             sem((2,)),
             sem((2,)),
+            sem((2, 2)),
             sem((2,)),
             sem((2, 2)),
             sem((2, 2)),

time: 67.1 us -> 65.6 us (0.978)
  Pallas kernels: 63.2 us -> 61.7 us
    pallas_call x1, Pallas kernels: 63.2 us -> 61.7 us  [local(): pl.pallas_call(functools.partial(block_kernel, n), out_shape=(out, out),...]
where the time goes in v4:
time: 65.6 us; the launch traced here: 65.5 us
  Pallas kernels  61.7 us (94%)
  local copies, waits for them, and re-layouts  3.14 us (5%)
    pallas_call x1, Pallas kernels, local(): pl.pallas_call(functools.partial(block_kernel, n), out_shape=(out, out),...  61.7 us
    unnamed x2, local copies, waits for them, and re-layouts  3.14 us

profile of v4, /device:TPU:1, one launch (start us, length us, event | category | flops | bytes accessed | tf_op | source)
XLA Modules:
  0.0 65.5 jit_solution(8018183693234316333)
XLA Ops:
  0.6 61.7 %shard_map.86 = (bf16[256,256]{1,0:T(8,128)(2,1)}, bf16[256,256]{1,0:T(8,128)(2,1)}) custom-call(bf16[256,256]{1,0:T(8,128)(2,1)} %tok.1, bf16[256,256]{1,0:T(8,128)(2,1)} %cot.1, bf16[3,1024,256]{2,1,0:T(8,128)(2,1)} %w_in_hbm.1, f32[3,3,256]{2,1,0:T(4,128)} %taps.1, f32[1,256]{1,0:T(1,128)} %bitcast.1, f32[256,256]{1,0:T(8,128)} %filt.1, ...), custom_call_target="tpu_custom_call" | custom-call | tf_op jit(solution)/shard_map/pallas_call | solution.py:354
  62.4 1.6 %copy.11 = bf16[256,256]{1,0:T(8,128)(2,1)} copy(bf16[256,256]{1,0:T(8,128)(2,1)} %get-tuple-element.4) | data formatting | bytes 262144
  63.9 1.6 %copy.12 = bf16[256,256]{1,0:T(8,128)(2,1)} copy(bf16[256,256]{1,0:T(8,128)(2,1)} %get-tuple-element.5) | data formatting | bytes 262144

commit v5 on v4

--- a/solution.py
+++ b/solution.py
@@ -30,12 +30,16 @@
     return jnp.where(col + (col // 4) * 4 + 4 * half == row, 1.0, 0.0).astype(BF16)
 
 
-def collect(pair):
-    row = lax.broadcasted_iota(jnp.int32, (1024, 512), 0)
-    col = lax.broadcasted_iota(jnp.int32, (1024, 512), 1)
-    channel = row % 256
-    source = (channel // 4) * 8 + 2 * (row // 256) + channel % 2
-    return jnp.where((col == source) & ((channel // 2) % 2 == pair), 1.0, 0.0).astype(BF16)
+def collect(pair, cs):
+    channel = lax.broadcasted_iota(jnp.int32, (256, 128), 0)
+    source = (channel // 4) * 8 + channel % 2
+    source = jnp.where((channel // 2) % 2 == pair, source, -1024)
+    for tile in range(4):
+        away = lax.broadcasted_iota(jnp.int32, (256, 128), 1) + 128 * tile - source
+        for part in range(4):
+            cs[pair, 256 * part : 256 * (part + 1), 128 * tile : 128 * (tile + 1)] = jnp.where(
+                away == 2 * part, 1.0, 0.0
+            ).astype(BF16)
 
 
 def chunks(spread_ref, value):
@@ -44,26 +48,28 @@
 
 
 def exchange(n, send_ref, recv_ref, offset, sems):
-    me = lax.axis_index("seq")
-
-    def one(j, carry):
-        to = lax.rem(me + j, n)
+    me, p = lax.axis_index("seq"), lax.axis_index("panel")
+    chip = p // 2
+    across = (1 - chip) * 2 + lax.rem(p, 2)
+    z, y, x = me // 16, lax.rem(me // 4, 4), lax.rem(me, 4)
+    hops = {0: 0, 1: 1, 2: 2, 3: 1}
+    steps = [(dz, dy, dx) for dz in (3, -3, 1, -1) for dy in range(4) for dx in range(4)]
+    steps.sort(key=lambda s: -(abs(s[0]) + hops[s[1]] + hops[s[2]]))
+    for dz, dy, dx in steps:
+        to_z = lax.rem(z + (dz - 1) // 2 + chip + 4, 4)
+        to = to_z * 16 + lax.rem(y + dy, 4) * 4 + lax.rem(x + dx, 4)
         pltpu.make_async_remote_copy(
             src_ref=send_ref.at[to],
             dst_ref=recv_ref.at[me + offset],
             send_sem=sems.at[0],
             recv_sem=sems.at[1],
-            device_id={"seq": to},
+            device_id={"seq": to, "panel": across},
             device_id_type=MESH,
         ).start()
-        return carry
-
-    lax.fori_loop(1, n, one, 0, unroll=9)
-    recv_ref[me + offset] = send_ref[me]
 
 
 def await_all(n, ref, sem):
-    part = ref.at[pl.ds(0, n - 1)]
+    part = ref.at[pl.ds(0, n)]
     pltpu.make_async_copy(part, part, sem).wait()
 
 
@@ -147,7 +153,7 @@
 def block_kernel(
     n, tok, cot, w_in_hbm, taps, skip, filt, w_out_hbm, out_ref, grad_ref,
     w_in, w_out, tokb, cotb, ext, gate, sig, gg, gs, es, cs, hs, hr, hf, hc, ss, sr, sf, gx, gr, gf, xl, r_ref, yf, ys, yr,
-    ups, edge, gp, own, half_send, half_recv, sum_send, sum_recv,
+    ups, edge, gp, own, other, half_send, half_recv, sum_send, sum_recv,
     wsem, tsem, fsem, esem, csem, hsem, ssem, gsem, ysem, usem, rsem, qsem,
 ):
     me, p = lax.axis_index("seq"), lax.axis_index("panel")
@@ -170,15 +176,15 @@
         )
 
     signal(me, sibling)
-    signal(me, across)
-    for other in (sibling, across, diagonal):
-        signal(earlier, other)
+    for peer in (p, sibling, diagonal):
+        signal(earlier, peer)
+    signal(later, p)
 
     def greet(j, carry):
-        signal(lax.rem(me + j, n), p)
+        signal(lax.rem(me + j, n), across)
         return carry
 
-    lax.fori_loop(1, n, greet, 0, unroll=9)
+    lax.fori_loop(0, n, greet, 0, unroll=8)
 
     def send(src, dst, sems, seq, panel):
         copy = pltpu.make_async_remote_copy(
@@ -192,29 +198,30 @@
         copy.start()
         return copy
 
-    pl.semaphore_wait(barrier, n + 4)
+    pl.semaphore_wait(barrier, n + 5)
 
     body = pl.ds(16, 256)
     rim = pl.ds(0, 16)
-    tok_across = send(tok, tokb.at[p, body], tsem.at[0], me, across)
-    tok_sibling = send(tok, tokb.at[p, body], tsem.at[1], me, sibling)
     edges = [
         send(tok.at[pl.ds(240, 16)], tokb.at[p, rim], esem.at[slot], later, panel)
         for slot, panel in enumerate((p, sibling, across, diagonal))
     ]
+    tok_across = send(tok, tokb.at[p, body], tsem.at[0], me, across)
+    tok_sibling = send(tok, tokb.at[p, body], tsem.at[1], me, sibling)
     es[...] = spread()
     hs[...] = chunks(es, filt[...].astype(BF16))
     hr[0] = jnp.zeros((8, 128), BF16)
-    exchange(n, hs, hr, 1, hsem)
+    tokb[p, 16:272, :] = tok[...]
+    cotb[p] = cot[...]
+    tok_across.wait_send()
     cot_across = send(cot, cotb.at[p], csem.at[0], me, across)
     cot_sibling = send(cot, cotb.at[p], csem.at[1], me, sibling)
-    tokb[p, 16:272, :] = tok[...]
-    cotb[p] = cot[...]
-    cs[0] = collect(0)
-    cs[1] = collect(1)
+    collect(0, cs)
+    collect(1, cs)
     eye, flip = identity(False), identity(True)
     tok_across.wait_recv()
     tok_forward = send(tokb.at[across, body], tokb.at[across, body], fsem.at[0], me, sibling)
+    exchange(n, hs, hr, 1, hsem)
     tok_sibling.wait_recv()
     for copy in edges:
         copy.wait_recv()
@@ -241,12 +248,6 @@
     sig[...] = gate[2] * gate[1]
     ss[...] = chunks(es, sig[...].astype(BF16))
     exchange(n, ss, sr, 0, ssem)
-    await_all(n, hr, hsem.at[1])
-    hf[...] = hr[...].astype(F32).reshape(520, 128)
-    for c in range(4):
-        hc[c] = hf[pl.ds(8 + c, 128, stride=4), :]
-    build_toeplitz(hc, r_ref, 0, 1)
-
     cot_across.wait_recv()
     cot_forward = send(cotb.at[across], cotb.at[across], fsem.at[1], me, sibling)
     cot_sibling.wait_recv()
@@ -267,7 +268,11 @@
     gx[...] = chunks(es, turned)
     exchange(n, gx, gr, 0, gsem)
 
-    build_toeplitz(hc, r_ref, 1, 4)
+    await_all(n, hr, hsem.at[1])
+    hf[...] = hr[...].astype(F32).reshape(520, 128)
+    for c in range(4):
+        hc[c] = hf[pl.ds(8 + c, 128, stride=4), :]
+    build_toeplitz(hc, r_ref, 0, 4)
     await_all(n, sr, ssem.at[1])
     await_all(n, gr, gsem.at[1])
     shifted_blocks(sr, gr, sf, gf, xl)
@@ -289,17 +294,21 @@
     ups[2, 0:256, :] = grad_signal * gate[1]
     rim_copy = send(ups.at[:, pl.ds(0, 8)], edge, usem, earlier, p)
 
-    def scatter_sum(which, product):
+    def send_halves(which, product):
         half_send[which, 0] = product(sibling).astype(BF16)
         half_send[which, 1] = product(diagonal).astype(BF16)
-        first = send(half_send.at[which], half_recv.at[which], rsem.at[which], me, sibling)
-        own[which] = product(p)
-        value = product(across)
+        return send(half_send.at[which], half_recv.at[which], rsem.at[which], me, sibling)
+
+    def send_sum(which, first):
         first.wait_recv()
-        sum_send[which] = (value + half_recv[which, 1].astype(F32)).astype(BF16)
-        second = send(sum_send.at[which], sum_recv.at[which], qsem.at[which], me, across)
-        own[which] = own[which] + half_recv[which, 0].astype(F32)
-        return first, second
+        value = other[which] + half_recv[which, 1].astype(F32)
+        sum_send[which] = value.astype(BF16)
+        return send(sum_send.at[which], sum_recv.at[which], qsem.at[which], me, across)
+
+    def finish(which, second):
+        second.wait_recv()
+        value = own[which] + half_recv[which, 0].astype(F32) + sum_recv[which].astype(F32)
+        return value.astype(BF16)
 
     gated = (state * gate[0]).astype(BF16)
 
@@ -307,7 +316,9 @@
         cols = pl.ds(pl.multiple_of(k * 256, 256), 256)
         return jnp.dot(gated, w_out[:, cols], preferred_element_type=F32)
 
-    sent = scatter_sum(0, out_product)
+    out_first = send_halves(0, out_product)
+    other[0] = out_product(across)
+    own[0] = out_product(p)
 
     rim_copy.wait_recv()
     ups[:, 256:264, :] = edge[...] * (me < n - 1).astype(F32)
@@ -328,15 +339,17 @@
             value = part if value is None else value + part
         return value
 
-    sent = sent + scatter_sum(1, grad_product)
-    sent[1].wait_recv()
-    out_ref[...] = (own[0] + sum_recv[0].astype(F32)).astype(BF16)
-    sent[3].wait_recv()
-    grad_ref[...] = (own[1] + sum_recv[1].astype(F32)).astype(BF16)
-
-    for copy in (tok_across, tok_sibling, tok_forward, cot_across, cot_sibling, cot_forward, rim_copy):
+    grad_first = send_halves(1, grad_product)
+    out_second = send_sum(0, out_first)
+    other[1] = grad_product(across)
+    grad_second = send_sum(1, grad_first)
+    own[1] = grad_product(p)
+    out_ref[...] = finish(0, out_second)
+    grad_ref[...] = finish(1, grad_second)
+
+    for copy in (tok_sibling, tok_forward, cot_across, cot_sibling, cot_forward, rim_copy):
         copy.wait_send()
-    for copy in tuple(edges) + sent:
+    for copy in tuple(edges) + (out_first, out_second, grad_first, grad_second):
         copy.wait_send()
     await_all(n, hr, hsem.at[0])
     await_all(n, sr, ssem.at[0])
@@ -387,6 +400,7 @@
             pltpu.VMEM((3, 8, 256), F32),
             pltpu.VMEM((3, 256, 256), BF16),
             pltpu.VMEM((2, 256, 256), F32),
+            pltpu.VMEM((2, 256, 256), F32),
             pltpu.VMEM((2, 2, 256, 256), BF16),
             pltpu.VMEM((2, 2, 256, 256), BF16),
             pltpu.VMEM((2, 256, 256), BF16),
@@ -405,7 +419,7 @@
             sem((2, 2)),
         ],
         compiler_params=pltpu.CompilerParams(
-            collective_id=0, has_side_effects=True, vmem_limit_bytes=58 * 2**20
+            collective_id=0, has_side_effects=True, vmem_limit_bytes=54 * 2**20
         ),
     )(
         tokens,

time: 65.6 us -> 61.1 us (0.931)
  Pallas kernels: 61.7 us -> 57.1 us
    pallas_call x1, Pallas kernels: 61.7 us -> 57.1 us  [local(): pl.pallas_call(functools.partial(block_kernel, n), out_shape=(out, out),...]
where the time goes in v5:
time: 61.1 us; the launch traced here: 60.8 us
  Pallas kernels  57.1 us (93%)
  local copies, waits for them, and re-layouts  3.14 us (5%)
  between operations  0.64 us (1%)
    pallas_call x1, Pallas kernels, local(): pl.pallas_call(functools.partial(block_kernel, n), out_shape=(out, out),...  57.1 us
    unnamed x2, local copies, waits for them, and re-layouts  3.14 us

profile of v5, /device:TPU:1, one launch (start us, length us, event | category | flops | bytes accessed | tf_op | source)
XLA Modules:
  0.0 60.8 jit_solution(3021513735400633433)
XLA Ops:
  0.6 57.1 %shard_map.86 = (bf16[256,256]{1,0:T(8,128)(2,1)}, bf16[256,256]{1,0:T(8,128)(2,1)}) custom-call(bf16[256,256]{1,0:T(8,128)(2,1)} %tok.1, bf16[256,256]{1,0:T(8,128)(2,1)} %cot.1, bf16[3,1024,256]{2,1,0:T(8,128)(2,1)} %w_in_hbm.1, f32[3,3,256]{2,1,0:T(4,128)} %taps.1, f32[1,256]{1,0:T(1,128)} %bitcast.1, f32[256,256]{1,0:T(8,128)} %filt.1, ...), custom_call_target="tpu_custom_call" | custom-call | tf_op jit(solution)/shard_map/pallas_call | solution.py:367
  57.7 1.6 %copy.11 = bf16[256,256]{1,0:T(8,128)(2,1)} copy(bf16[256,256]{1,0:T(8,128)(2,1)} %get-tuple-element.4) | data formatting | bytes 262144
  59.3 1.6 %copy.12 = bf16[256,256]{1,0:T(8,128)(2,1)} copy(bf16[256,256]{1,0:T(8,128)(2,1)} %get-tuple-element.5) | data formatting | bytes 262144

commit v6 on v5

--- a/solution.py
+++ b/solution.py
@@ -79,15 +79,13 @@
     cut = col >= 128 - row
 
     def channel(c, carry):
-        r_ref[c, 128:256, 0:128] = jnp.zeros((128, 128), BF16)
+        r_ref[c, :, 0:128] = jnp.zeros((128, 128), BF16)
         early = jnp.zeros((128, 128), F32)
         for k in range(128):
             now = jnp.broadcast_to(hc[c, k : k + 1, :], (128, 128))
             mixed = jnp.where(cut, early, now)
             tile = pltpu.roll(mixed, 0, 1, stride=1, stride_axis=0).astype(BF16)
-            at = 128 * k
-            r_ref[c, 0:128, at : at + 128] = tile
-            r_ref[c, 128:256, at + 128 : at + 256] = tile
+            r_ref[c, :, 128 * (k + 1) : 128 * (k + 2)] = tile
             early = now
         return carry
 
@@ -123,10 +121,11 @@
             z = None
             for q in range(8):
                 at = (8 * q + r) * 256
+                lags = jnp.concatenate(
+                    [r_ref[c, :, at + 128 : at + 384], r_ref[c, :, at : at + 256]], axis=0
+                )
                 part = jnp.dot(
-                    xl[c, :, 256 * q : 256 * (q + 1)],
-                    r_ref[c, :, at : at + 256],
-                    preferred_element_type=F32,
+                    xl[c, :, 256 * q : 256 * (q + 1)], lags, preferred_element_type=F32
                 )
                 z = part if z is None else z + part
             z = z.reshape(8, 2, 8, 256)
@@ -151,9 +150,9 @@
 
 
 def block_kernel(
-    n, tok, cot, w_in_hbm, taps, skip, filt, w_out_hbm, out_ref, grad_ref,
-    w_in, w_out, tokb, cotb, ext, gate, sig, gg, gs, es, cs, hs, hr, hf, hc, ss, sr, sf, gx, gr, gf, xl, r_ref, yf, ys, yr,
-    ups, edge, gp, own, other, half_send, half_recv, sum_send, sum_recv,
+    n, tok, cot, w_in_hbm, taps, skip, filt_hbm, w_out_hbm, out_ref,
+    filt, w_in, w_out, tokb, cotb, ext, gate, sig, gg, gs, es, cs, hs, hr, hf, hc, ss, sr, sf, gx, gr, gf, xl, r_ref, yf, ys, yr,
+    ups, head, edge, gp, own, other, half_send, half_recv, sum_send, sum_recv,
     wsem, tsem, fsem, esem, csem, hsem, ssem, gsem, ysem, usem, rsem, qsem,
 ):
     me, p = lax.axis_index("seq"), lax.axis_index("panel")
@@ -165,8 +164,13 @@
 
     load_in = pltpu.make_async_copy(w_in_hbm, w_in, wsem.at[0])
     load_out = pltpu.make_async_copy(w_out_hbm, w_out, wsem.at[1])
-    load_in.start()
-    load_out.start()
+    body = pl.ds(16, 256)
+    rim = pl.ds(0, 16)
+    load_filter = pltpu.make_async_copy(filt_hbm, filt, wsem.at[2])
+    load_tok = pltpu.make_async_copy(tok, tokb.at[p, body], wsem.at[3])
+    load_cot = pltpu.make_async_copy(cot, cotb.at[p], wsem.at[4])
+    for load in (load_filter, load_tok, load_cot, load_in, load_out):
+        load.start()
 
     barrier = pltpu.get_barrier_semaphore()
 
@@ -200,8 +204,6 @@
 
     pl.semaphore_wait(barrier, n + 5)
 
-    body = pl.ds(16, 256)
-    rim = pl.ds(0, 16)
     edges = [
         send(tok.at[pl.ds(240, 16)], tokb.at[p, rim], esem.at[slot], later, panel)
         for slot, panel in enumerate((p, sibling, across, diagonal))
@@ -209,10 +211,9 @@
     tok_across = send(tok, tokb.at[p, body], tsem.at[0], me, across)
     tok_sibling = send(tok, tokb.at[p, body], tsem.at[1], me, sibling)
     es[...] = spread()
+    load_filter.wait()
     hs[...] = chunks(es, filt[...].astype(BF16))
     hr[0] = jnp.zeros((8, 128), BF16)
-    tokb[p, 16:272, :] = tok[...]
-    cotb[p] = cot[...]
     tok_across.wait_send()
     cot_across = send(cot, cotb.at[p], csem.at[0], me, across)
     cot_sibling = send(cot, cotb.at[p], csem.at[1], me, sibling)
@@ -227,6 +228,7 @@
         copy.wait_recv()
     tok_forward.wait_recv()
     load_in.wait()
+    load_tok.wait()
 
     started = (me > 0).astype(F32)
     for j in range(3):
@@ -253,6 +255,7 @@
     cot_sibling.wait_recv()
     cot_forward.wait_recv()
     load_out.wait()
+    load_cot.wait()
     value = None
     for k in range(4):
         part = lax.dot_general(
@@ -287,12 +290,14 @@
     back = back.astype(BF16)
     state = jnp.concatenate([back[0:256], back[512:768]], axis=1)
     grad_signal = jnp.concatenate([back[256:512], back[768:1024]], axis=1)
+    head_state = turn(eye[0:8], state) + skip[...] * sig[0:8, :]
+    head_grad = turn(flip[0:8], grad_signal) + skip[...] * gs[0:8, :]
+    head[0] = gg[0:8, :] * head_state
+    head[1] = head_grad * gate[2, 0:8, :]
+    head[2] = head_grad * gate[1, 0:8, :]
+    rim_copy = send(head, edge, usem, earlier, p)
     state = turn(eye, state) + skip[...] * sig[...]
     grad_signal = turn(flip, grad_signal) + skip[...] * gs[...]
-    ups[0, 0:256, :] = gg[...] * state
-    ups[1, 0:256, :] = grad_signal * gate[2]
-    ups[2, 0:256, :] = grad_signal * gate[1]
-    rim_copy = send(ups.at[:, pl.ds(0, 8)], edge, usem, earlier, p)
 
     def send_halves(which, product):
         half_send[which, 0] = product(sibling).astype(BF16)
@@ -318,7 +323,11 @@
 
     out_first = send_halves(0, out_product)
     other[0] = out_product(across)
+    ups[0, 0:256, :] = gg[...] * state
+    ups[1, 0:256, :] = grad_signal * gate[2]
+    ups[2, 0:256, :] = grad_signal * gate[1]
     own[0] = out_product(p)
+    out_second = send_sum(0, out_first)
 
     rim_copy.wait_recv()
     ups[:, 256:264, :] = edge[...] * (me < n - 1).astype(F32)
@@ -340,12 +349,11 @@
         return value
 
     grad_first = send_halves(1, grad_product)
-    out_second = send_sum(0, out_first)
     other[1] = grad_product(across)
     grad_second = send_sum(1, grad_first)
     own[1] = grad_product(p)
-    out_ref[...] = finish(0, out_second)
-    grad_ref[...] = finish(1, grad_second)
+    out_ref[0] = finish(0, out_second)
+    out_ref[1] = finish(1, grad_second)
 
     for copy in (tok_sibling, tok_forward, cot_across, cot_sibling, cot_forward, rim_copy):
         copy.wait_send()
@@ -360,16 +368,16 @@
 
 def local(tokens, cotangent, in_weight, short_kernel, skip_gain, long_filter, out_weight):
     n = lax.axis_size("seq")
-    out = jax.ShapeDtypeStruct((256, 256), BF16)
     vmem = pl.BlockSpec(memory_space=pltpu.VMEM)
-    hbm = pl.BlockSpec(memory_space=pl.ANY)
+    hbm = pl.BlockSpec(memory_space=pltpu.HBM)
     sem = pltpu.SemaphoreType.DMA
-    return pl.pallas_call(
+    both = pl.pallas_call(
         functools.partial(block_kernel, n),
-        out_shape=(out, out),
-        in_specs=[vmem, vmem, hbm, vmem, vmem, vmem, hbm],
-        out_specs=(vmem, vmem),
+        out_shape=jax.ShapeDtypeStruct((2, 256, 256), BF16),
+        in_specs=[hbm, hbm, hbm, vmem, vmem, hbm, hbm],
+        out_specs=vmem,
         scratch_shapes=[
+            pltpu.VMEM((256, 256), F32),
             pltpu.VMEM((3, 1024, 256), BF16),
             pltpu.VMEM((256, 1024), BF16),
             pltpu.VMEM((4, 272, 256), BF16),
@@ -392,11 +400,12 @@
             pltpu.VMEM((64, 8, 128), BF16),
             pltpu.VMEM((512, 128), F32),
             pltpu.VMEM((4, 128, 2048), BF16),
-            pltpu.VMEM((4, 256, 16384 + 128), BF16),
+            pltpu.VMEM((4, 128, 16384 + 128), BF16),
             pltpu.VMEM((512, 128), F32),
             pltpu.VMEM((2, 64, 8, 128), BF16),
             pltpu.VMEM((2, 64, 8, 128), BF16),
             pltpu.VMEM((3, 264, 256), F32),
+            pltpu.VMEM((3, 8, 256), F32),
             pltpu.VMEM((3, 8, 256), F32),
             pltpu.VMEM((3, 256, 256), BF16),
             pltpu.VMEM((2, 256, 256), F32),
@@ -405,7 +414,7 @@
             pltpu.VMEM((2, 2, 256, 256), BF16),
             pltpu.VMEM((2, 256, 256), BF16),
             pltpu.VMEM((2, 256, 256), BF16),
-            sem((2,)),
+            sem((5,)),
             sem((2, 2)),
             sem((2, 2)),
             sem((4, 2)),
@@ -419,7 +428,7 @@
             sem((2, 2)),
         ],
         compiler_params=pltpu.CompilerParams(
-            collective_id=0, has_side_effects=True, vmem_limit_bytes=54 * 2**20
+            collective_id=0, has_side_effects=True, vmem_limit_bytes=55 * 2**20
         ),
     )(
         tokens,
@@ -430,6 +439,7 @@
         long_filter,
         out_weight,
     )
+    return both[0], both[1]
 
 
 def solution(mesh):

time: 61.1 us -> 59.8 us (0.979)
  local copies, waits for them, and re-layouts: 3.14 us -> 1.68 us
    unnamed x2 -> x0, local copies, waits for them, and re-layouts: 3.14 us -> none
    squeeze x0 -> x1, local copies, waits for them, and re-layouts: none -> 1.68 us  [local(): return (both[0], both[1])]
where the time goes in v6:
time: 59.8 us; the launch traced here: 59.6 us
  Pallas kernels  57.3 us (96%)
  local copies, waits for them, and re-layouts  1.68 us (3%)
  between operations  0.64 us (1%)
    pallas_call x1, Pallas kernels, local(): pl.pallas_call(functools.partial(block_kernel, n), out_shape=jax.ShapeDty...  57.3 us
    squeeze x1, local copies, waits for them, and re-layouts, local(): return (both[0], both[1])  1.68 us

profile of v6, /device:TPU:1, one launch (start us, length us, event | category | flops | bytes accessed | tf_op | source)
XLA Modules:
  0.0 59.6 jit_solution(13097440825795297673)
XLA Ops:
  0.6 57.3 %shard_map.86 = bf16[2,256,256]{2,1,0:T(8,128)(2,1)} custom-call(bf16[256,256]{1,0:T(8,128)(2,1)} %tok.1, bf16[256,256]{1,0:T(8,128)(2,1)} %cot.1, bf16[3,1024,256]{2,1,0:T(8,128)(2,1)} %w_in_hbm.1, f32[3,3,256]{2,1,0:T(4,128)} %taps.1, f32[1,256]{1,0:T(1,128)} %bitcast.5, f32[256,256]{1,0:T(8,128)} %filt_hbm.1, bf16[256,1024]{1,0:T(8,128)(2,1)} %w_out_hbm.1), custom_call_target="tpu_custom_call" | custom-call | tf_op jit(solution)/shard_map/pallas_call | solution.py:374
  58.0 1.7 %slice_bitcast_fusion = (bf16[256,256]{1,0:T(8,128)(2,1)}, bf16[256,256]{1,0:T(8,128)(2,1)}) fusion(bf16[2,256,256]{2,1,0:T(8,128)(2,1)} %shard_map.86), kind=kLoop, calls=%fused_computation | loop fusion | bytes 524288 | tf_op jit(solution)/shard_map/squeeze | solution.py:442

commit v7 on v6

--- a/solution.py
+++ b/solution.py
@@ -373,7 +373,7 @@
     sem = pltpu.SemaphoreType.DMA
     both = pl.pallas_call(
         functools.partial(block_kernel, n),
-        out_shape=jax.ShapeDtypeStruct((2, 256, 256), BF16),
+        out_shape=pltpu.VMEM((2, 256, 256), BF16),
         in_specs=[hbm, hbm, hbm, vmem, vmem, hbm, hbm],
         out_specs=vmem,
         scratch_shapes=[

time: 59.8 us -> 58.1 us (0.972)
  local copies, waits for them, and re-layouts: 1.68 us -> 0.72 us
  Pallas kernels: 57.3 us -> 56.6 us
    squeeze x1, local copies, waits for them, and re-layouts: 1.68 us -> 0.72 us  [local(): return (both[0], both[1])]
    pallas_call x1, Pallas kernels: 57.3 us -> 56.6 us  [local(): pl.pallas_call(functools.partial(block_kernel, n), out_shape=pltpu.VMEM((...]
where the time goes in v7:
time: 58.1 us; the launch traced here: 58 us
  Pallas kernels  56.6 us (97%)
  local copies, waits for them, and re-layouts  0.72 us (1%)
  between operations  0.64 us (1%)
    pallas_call x1, Pallas kernels, local(): pl.pallas_call(functools.partial(block_kernel, n), out_shape=pltpu.VMEM((...  56.6 us

profile of v7, /device:TPU:1, one launch (start us, length us, event | category | flops | bytes accessed | tf_op | source)
XLA Modules:
  0.0 58.0 jit_solution(4893714560302116528)
XLA Ops:
  0.6 56.6 %shard_map.86 = bf16[2,256,256]{2,1,0:T(8,128)(2,1)S(1)} custom-call(bf16[256,256]{1,0:T(8,128)(2,1)} %tok.1, bf16[256,256]{1,0:T(8,128)(2,1)} %cot.1, bf16[3,1024,256]{2,1,0:T(8,128)(2,1)} %w_in_hbm.1, f32[3,3,256]{2,1,0:T(4,128)} %taps.1, f32[1,256]{1,0:T(1,128)} %bitcast.5, f32[256,256]{1,0:T(8,128)} %filt_hbm.1, bf16[256,1024]{1,0:T(8,128)(2,1)} %w_out_hbm.1), custom_call_target="tpu_custom_call" | custom-call | tf_op jit(solution)/shard_map/pallas_call | solution.py:374
  57.3 0.7 %slice_bitcast_fusion = (bf16[256,256]{1,0:T(8,128)(2,1)}, bf16[256,256]{1,0:T(8,128)(2,1)}) fusion(bf16[2,256,256]{2,1,0:T(8,128)(2,1)S(1)} %shard_map.86), kind=kLoop, calls=%fused_computation | loop fusion | bytes 524288 | tf_op jit(solution)/shard_map/squeeze | solution.py:442

commit v8 on v7

--- a/solution.py
+++ b/solution.py
@@ -107,7 +107,6 @@
         x = jnp.concatenate(rows, axis=0).astype(BF16)
         xl[c, :, 0:256] = x
         for q in range(1, 8):
-            xl[c, 0 : 16 * q, 256 * q : 256 * (q + 1)] = jnp.zeros((16 * q, 256), BF16)
             xl[c, 16 * q :, 256 * q : 256 * (q + 1)] = x[: 128 - 16 * q]
 
 
@@ -210,13 +209,12 @@
     ]
     tok_across = send(tok, tokb.at[p, body], tsem.at[0], me, across)
     tok_sibling = send(tok, tokb.at[p, body], tsem.at[1], me, sibling)
+    cot_across = send(cot, cotb.at[p], csem.at[0], me, across)
+    cot_sibling = send(cot, cotb.at[p], csem.at[1], me, sibling)
     es[...] = spread()
     load_filter.wait()
     hs[...] = chunks(es, filt[...].astype(BF16))
     hr[0] = jnp.zeros((8, 128), BF16)
-    tok_across.wait_send()
-    cot_across = send(cot, cotb.at[p], csem.at[0], me, across)
-    cot_sibling = send(cot, cotb.at[p], csem.at[1], me, sibling)
     collect(0, cs)
     collect(1, cs)
     eye, flip = identity(False), identity(True)
@@ -231,7 +229,7 @@
     load_tok.wait()
 
     started = (me > 0).astype(F32)
-    for j in range(3):
+    def branch(j):
         value = None
         for k in range(4):
             part = jnp.dot(
@@ -241,15 +239,18 @@
         value = value.astype(BF16).astype(F32)
         ext[j, 0:16, :] = value[0:16] * started
         ext[j, 16:272, :] = value[16:]
-    for j in range(3):
         gate[j] = (
             taps[0, j : j + 1, :] * ext[j, 16:272, :]
             + taps[1, j : j + 1, :] * ext[j, 15:271, :]
             + taps[2, j : j + 1, :] * ext[j, 14:270, :]
         )
+
+    branch(1)
+    branch(2)
     sig[...] = gate[2] * gate[1]
     ss[...] = chunks(es, sig[...].astype(BF16))
     exchange(n, ss, sr, 0, ssem)
+    branch(0)
     cot_across.wait_recv()
     cot_forward = send(cotb.at[across], cotb.at[across], fsem.at[1], me, sibling)
     cot_sibling.wait_recv()
@@ -276,6 +277,9 @@
     for c in range(4):
         hc[c] = hf[pl.ds(8 + c, 128, stride=4), :]
     build_toeplitz(hc, r_ref, 0, 4)
+    for c in range(4):
+        for q in range(1, 8):
+            xl[c, 0 : 16 * q, 256 * q : 256 * (q + 1)] = jnp.zeros((16 * q, 256), BF16)
     await_all(n, sr, ssem.at[1])
     await_all(n, gr, gsem.at[1])
     shifted_blocks(sr, gr, sf, gf, xl)
@@ -355,7 +359,7 @@
     out_ref[0] = finish(0, out_second)
     out_ref[1] = finish(1, grad_second)
 
-    for copy in (tok_sibling, tok_forward, cot_across, cot_sibling, cot_forward, rim_copy):
+    for copy in (tok_across, tok_sibling, tok_forward, cot_across, cot_sibling, cot_forward, rim_copy):
         copy.wait_send()
     for copy in tuple(edges) + (out_first, out_second, grad_first, grad_second):
         copy.wait_send()

time: 58.1 us -> 57.6 us (level)
  no operation moved by 1% of the time
where the time goes in v8:
time: 57.6 us; the launch traced here: 57.4 us
  Pallas kernels  56.1 us (97%)
  local copies, waits for them, and re-layouts  0.72 us (1%)
  between operations  0.64 us (1%)
    pallas_call x1, Pallas kernels, local(): pl.pallas_call(functools.partial(block_kernel, n), out_shape=pltpu.VMEM((...  56.1 us

profile of v8, /device:TPU:1, one launch (start us, length us, event | category | flops | bytes accessed | tf_op | source)
XLA Modules:
  0.0 57.4 jit_solution(14509141187375794708)
XLA Ops:
  0.6 56.1 %shard_map.86 = bf16[2,256,256]{2,1,0:T(8,128)(2,1)S(1)} custom-call(bf16[256,256]{1,0:T(8,128)(2,1)} %tok.1, bf16[256,256]{1,0:T(8,128)(2,1)} %cot.1, bf16[3,1024,256]{2,1,0:T(8,128)(2,1)} %w_in_hbm.1, f32[3,3,256]{2,1,0:T(4,128)} %taps.1, f32[1,256]{1,0:T(1,128)} %bitcast.5, f32[256,256]{1,0:T(8,128)} %filt_hbm.1, bf16[256,1024]{1,0:T(8,128)(2,1)} %w_out_hbm.1), custom_call_target="tpu_custom_call" | custom-call | tf_op jit(solution)/shard_map/pallas_call | solution.py:378
  56.7 0.7 %slice_bitcast_fusion = (bf16[256,256]{1,0:T(8,128)(2,1)}, bf16[256,256]{1,0:T(8,128)(2,1)}) fusion(bf16[2,256,256]{2,1,0:T(8,128)(2,1)S(1)} %shard_map.86), kind=kLoop, calls=%fused_computation | loop fusion | bytes 524288 | tf_op jit(solution)/shard_map/squeeze | solution.py:446
